TPU v7x, 256 devices: a whole 4x4x8 slice. The times are simulated.
256 devices in a mesh: sta: 8 (over x, core), cel: 32 (over z, y).
Axes of the slice: x: 4, y: 4, z: 8, core: 2. Of those that a mesh axis runs over, the one named last changes fastest.
Arguments:
- model_vectors: bfloat16 [16, 262144], P('sta', 'cel'), may hold values from -6 to 6
- station_xyz: float32 [3, 262144], P(None, 'sta'), may hold values from 0 to 2, as said below
- cell_xyz: float32 [3, 262144], P(None, 'cel'), may hold values from -1 to 2, as said below
- weights: float32 [262144], P('sta'), may hold values from 0.25 to 4
- near_pairs: int32 [8, 32, 64, 2], P('sta', 'cel'), may hold values from 0 to 127, as said below
- near_count: int32 [8, 32], P('sta'), may hold values from 8 to 64, as said below
- mid_pairs: int32 [8, 32, 128, 2], P('sta', 'cel'), may hold values from 0 to 127, as said below
- mid_u: bfloat16 [8, 32, 128, 32, 256], P('sta', 'cel'), may hold values from -0.375 to 0.375
- mid_v: bfloat16 [8, 32, 128, 32, 256], P('sta', 'cel'), may hold values from -0.375 to 0.375
Outputs:
- predicted: float32 [16, 262144], P(None, ('sta', 'cel'))
- gradient: float32 [16, 262144], P('sta', 'cel')
Inputs may be any that keep to these rules, and one draw needn't show every extreme that they name: `near_pairs`: entry 0 of a pair is a station tile below 128, entry 1 a cell tile below 32; a device's near and mid pairs are all different; slots at or past the device's near_count are ignored. `mid_pairs`: entry 0 a station tile below 128, entry 1 a cell tile below 32. `near_count`: each count is 64 divided by 1, 2, 4 or 8; some device has 64. `station_xyz`: east and north lie in 0 to 2; heights in 0.5 to 1. `cell_xyz`: east and north lie in 0 to 2; heights in -1 to -0.25.
All inputs are finite; a program needn't handle non-finite values.
Results may differ from a plain program's by a relative error of at most 0.015.
Values may be sent and summed in bfloat16 or wider, within the bound.
No kernel may reach another device: no remote copies, remote signals or barrier semaphores. Data moves between devices by JAX's collectives and lax.ppermute only.
A program may use at most 128 MiB of HBM per device.

v0:
```python
import functools

import jax
import jax.numpy as jnp
from jax import lax
from jax.experimental import pallas as pl
from jax.experimental.pallas import tpu as pltpu
from jax.sharding import PartitionSpec as P

VOLUME = 0.03125
FIELD = (0.17101, 0.46985, -0.86603)
ROOT = (3.0 * VOLUME) ** 0.5

TILE = 256
VECS = 16
GROUP = 8
MIB = 1 << 20
WIDE = 8
TALL = 4
HALF = 4
F32 = jnp.float32
BF16 = jnp.bfloat16

SMEM = pl.BlockSpec(memory_space=pltpu.SMEM)
VMEM = pl.BlockSpec(memory_space=pltpu.VMEM)
HBM = pl.BlockSpec(memory_space=pltpu.HBM)


def split3(x):
    high = x.astype(BF16).astype(F32)
    rest = x - high
    middle = rest.astype(BF16).astype(F32)
    return high, middle, rest - middle


def stack(lines, values):
    total = jnp.zeros(lines.shape, F32)
    for line, value in values:
        total = jnp.where(lines == line, value, total)
    return total


def field_of(x, y, z):
    return ROOT * (FIELD[0] * x + FIELD[1] * y + FIELD[2] * z)


def near_group(g, pairs, stations, features, out, first):
    lines = lax.broadcasted_iota(jnp.int32, (8, TILE), 0)
    for j in range(GROUP):
        at = lanes_of(pairs[0, g * GROUP + j])
        x, y, z = (stations[d : d + 1, at] for d in range(3))
        one = jnp.ones_like(x)
        wide = stack(lines, ((0, x), (1, y), (2, z), (3, x * x + y * y + z * z), (5, one)))
        flat = stack(lines, ((3, field_of(x, y, z)), (6, one)))
        left = features[pairs[1, g * GROUP + j]]

        def product(block):
            h, m, l = split3(block)
            right = jnp.concatenate((h, m, l, h, m, h), axis=0).astype(BF16)
            return jnp.dot(left, right, preferred_element_type=F32)

        inverse = lax.rsqrt(product(wide))
        along = product(flat)
        square = inverse * inverse
        out[(g - first) * GROUP + j] = (
            (along * along * square - VOLUME) * (square * inverse)
        ).astype(BF16)


def near_first_kernel(counts, pairs, station_hbm, cell_hbm, out, features, stations, cells, sem):
    fetches = [
        pltpu.make_async_copy(cell_hbm, cells, sem.at[0]),
        pltpu.make_async_copy(station_hbm, stations, sem.at[1]),
    ]
    for fetch in fetches:
        fetch.start()
    fetches[0].wait()

    def cell_chunk(i, carry):
        lines = lax.broadcasted_iota(jnp.int32, (8, TILE), 0)
        for q in range(4):
            at = lanes_of(i * 4 + q)
            x, y, z = (cells[d : d + 1, at] for d in range(3))
            square = x * x + y * y + z * z
            block = stack(
                lines,
                (
                    (0, -2.0 * x),
                    (1, -2.0 * y),
                    (2, -2.0 * z),
                    (3, jnp.ones_like(x)),
                    (5, square),
                    (6, -field_of(x, y, z)),
                ),
            )
            h, m, l = split3(block)
            features[i * 4 + q] = jnp.concatenate((h, h, h, m, m, l), axis=0).T.astype(BF16)
        return carry

    lax.fori_loop(0, features.shape[0] // 4, cell_chunk, 0)
    fetches[1].wait()

    def step(g, carry):
        near_group(g, pairs, stations, features, out, 0)
        return carry

    lax.fori_loop(0, jnp.minimum(near_groups(counts), HALF), step, 0)


def near_second_kernel(counts, pairs, stations, features, out):
    def step(g, carry):
        near_group(g, pairs, stations, features, out, HALF)
        return carry

    lax.fori_loop(HALF, near_groups(counts), step, 0)


def block_mask():
    lines = lax.broadcasted_iota(jnp.int32, (GROUP * VECS, TILE), 0) // VECS
    lanes = lax.broadcasted_iota(jnp.int32, (GROUP * VECS, TILE), 1) // (TILE // GROUP)
    return lines == lanes


def near_groups(counts):
    return counts[0, lax.axis_index("cel")] // GROUP


def contract(a, b, dim):
    return lax.dot_general(a, b, (((1,), (dim,)), ((), ())), preferred_element_type=F32)


def lanes_of(column):
    return pl.ds(pl.multiple_of(column * TILE, TILE), TILE)


def place(row):
    share = row >> 2
    return (share & (WIDE - 1)) * TALL + (share >> 3), lanes_of(row & 3)


def forward_kernel(counts, near, mid, *refs):
    parts = refs[:4]
    u_ref, v_ref, first_blocks, second_blocks, out, stacked, vectors, total = refs[4:]
    for k in range(4):
        stacked[4 * k : 4 * k + 4, :] = parts[k][...].astype(F32)
    vectors[...] = stacked[...].astype(BF16)
    total[...] = jnp.zeros_like(total)
    mask = block_mask()

    sums = []
    for g in range(u_ref.shape[0]):
        source = jnp.concatenate(
            [vectors[:, lanes_of(mid[1, g * GROUP + j])] for j in range(GROUP)], axis=0
        )
        reduced = contract(source, v_ref[g], 1)
        reduced = jnp.where(mask, reduced, 0.0).astype(BF16)
        sums.append(contract(reduced, u_ref[g], 0))
    for g in range(u_ref.shape[0]):
        for j in range(GROUP):
            slot, lanes = place(mid[0, g * GROUP + j])
            total[slot, :, lanes] += sums[g][j * VECS : (j + 1) * VECS]

    def near_step(g, carry, blocks, first):
        sums = [
            contract(vectors[:, lanes_of(near[1, g * GROUP + j])], blocks[(g - first) * GROUP + j], 0)
            for j in range(GROUP)
        ]
        for j in range(GROUP):
            slot, lanes = place(near[0, g * GROUP + j])
            total[slot, :, lanes] += sums[j]
        return carry

    groups = near_groups(counts)
    first_step = functools.partial(near_step, blocks=first_blocks, first=0)
    second_step = functools.partial(near_step, blocks=second_blocks, first=HALF)
    lax.fori_loop(0, jnp.minimum(groups, HALF), first_step, 0)
    lax.fori_loop(HALF, groups, second_step, 0)
    out[...] = total[...].astype(BF16)


def sum_of(parts):
    total = parts[0].astype(F32)
    for k in range(1, parts.shape[0]):
        total = total + parts[k].astype(F32)
    return total


def share_sum_kernel(parts, out):
    out[...] = sum_of(parts).astype(BF16)


def weigh_kernel(parts, weights, predicted, weighted):
    sta, cel = lax.axis_index("sta"), lax.axis_index("cel")
    total = sum_of(parts)
    share = weights[pl.ds(pl.multiple_of(cel * 8, 8), 8), :]
    for r in range(8):
        at = slice(r * 128, (r + 1) * 128)
        value = (total[:, at] * share[r : r + 1, :]).astype(BF16)
        for k in range(TALL):
            weighted[k, :, at] = value
    for place_of in range(8):

        @pl.when(sta == place_of)
        def _():
            for k in range(8):
                line = 2 * (k ^ place_of)
                predicted[line : line + 2, :] = total[2 * k : 2 * k + 2]


def copies_kernel(column, out):
    for i in range(WIDE):
        out[i] = column[...]


def adjoint_kernel(
    counts, near, mid, data, u_ref, v_ref, first_blocks, second_blocks, kept, swapped, total
):
    total[...] = jnp.zeros_like(total)
    mask = block_mask()

    def station_tile(row):
        slot, lanes = place(row)
        return data[slot, :, lanes]

    sums = []
    for g in range(u_ref.shape[0]):
        source = jnp.concatenate(
            [station_tile(mid[0, g * GROUP + j]) for j in range(GROUP)], axis=0
        )
        pulled = contract(source, u_ref[g], 1)
        pulled = jnp.where(mask, pulled, 0.0).astype(BF16)
        sums.append(contract(pulled, v_ref[g], 0))
    for g in range(u_ref.shape[0]):
        for j in range(GROUP):
            lanes = lanes_of(mid[1, g * GROUP + j])
            total[:, lanes] += sums[g][j * VECS : (j + 1) * VECS]

    def near_step(g, carry, blocks, first):
        sums = [
            contract(station_tile(near[0, g * GROUP + j]), blocks[(g - first) * GROUP + j], 1)
            for j in range(GROUP)
        ]
        for j in range(GROUP):
            total[:, lanes_of(near[1, g * GROUP + j])] += sums[j]
        return carry

    groups = near_groups(counts)
    first_step = functools.partial(near_step, blocks=first_blocks, first=0)
    second_step = functools.partial(near_step, blocks=second_blocks, first=HALF)
    lax.fori_loop(0, jnp.minimum(groups, HALF), first_step, 0)
    lax.fori_loop(HALF, groups, second_step, 0)
    for t in range(4):
        kept[2 * t : 2 * t + 2, :] = total[4 * t : 4 * t + 2, :]
    swapped[...] = jnp.concatenate(
        [total[4 * t + 2 : 4 * t + 4, :] for t in range(4)], axis=0
    ).astype(BF16)


def chip_sum_kernel(kept, swapped, *outs):
    total = kept[...] + swapped[...].astype(F32)
    for t in range(4):
        outs[t][...] = total[2 * t : 2 * t + 2].astype(outs[t].dtype)


def params(mib):
    return pltpu.CompilerParams(vmem_limit_bytes=mib * MIB)


def body(
    model_vectors, station_xyz, cell_xyz, weights, near_pairs, near_count, mid_pairs, mid_u, mid_v
):
    slots = near_pairs.shape[2]
    near = near_pairs[0, 0].T
    mid = mid_pairs[0, 0].T
    u_factor = mid_u.reshape(-1, TILE, TILE)
    v_factor = mid_v.reshape(-1, TILE, TILE)

    def over_sta(x, k):
        return lax.ppermute(x, "sta", [(i, i ^ k) for i in range(8)])

    wide_groups = [[WIDE * h + w for w in range(WIDE)] for h in range(TALL)]
    tall_groups = [[WIDE * h + w for h in range(TALL)] for w in range(WIDE)]

    def trade(x, axis, groups):
        return lax.all_to_all(x, axis, 0, 0, axis_index_groups=groups)

    half = HALF * GROUP
    cell_tiles = cell_xyz.shape[1] // TILE
    other_vectors = over_sta(model_vectors, 1)
    first_blocks, features, stations = pl.pallas_call(
        near_first_kernel,
        in_specs=[SMEM] * 2 + [HBM] * 2,
        out_specs=[VMEM] * 3,
        out_shape=[
            jax.ShapeDtypeStruct((half, TILE, TILE), BF16),
            jax.ShapeDtypeStruct((cell_tiles, TILE, 48), BF16),
            jax.ShapeDtypeStruct(station_xyz.shape, F32),
        ],
        scratch_shapes=[pltpu.VMEM(cell_xyz.shape, F32), pltpu.SemaphoreType.DMA((2,))],
        compiler_params=params(16),
        cost_estimate=pl.CostEstimate(
            flops=half * 2 * 512 * 48 * 256, bytes_accessed=6 * MIB, transcendentals=half * 65536
        ),
        name="near_first",
    )(near_count, near, station_xyz, cell_xyz)
    other_vectors, features = lax.optimization_barrier((other_vectors, features))
    chip_vectors = jnp.concatenate((model_vectors, other_vectors), axis=0)
    vector_parts = [chip_vectors] + [over_sta(chip_vectors, 2 * k) for k in range(1, 4)]
    second_blocks = pl.pallas_call(
        near_second_kernel,
        in_specs=[SMEM] * 2 + [VMEM] * 2,
        out_specs=VMEM,
        out_shape=jax.ShapeDtypeStruct((slots - half, TILE, TILE), BF16),
        compiler_params=params(16),
        cost_estimate=pl.CostEstimate(
            flops=half * 2 * 512 * 48 * 256, bytes_accessed=6 * MIB, transcendentals=half * 65536
        ),
        name="near_second",
    )(near_count, near, stations, features)

    wide = jax.ShapeDtypeStruct((WIDE, TALL, VECS, 1024), BF16)
    tall = jax.ShapeDtypeStruct((TALL, VECS, 1024), BF16)
    shares = pl.pallas_call(
        forward_kernel,
        in_specs=[SMEM] * 3 + [VMEM] * 8,
        out_specs=VMEM,
        out_shape=jax.ShapeDtypeStruct((32, VECS, 1024), BF16),
        scratch_shapes=[
            pltpu.VMEM((VECS, 8192), F32),
            pltpu.VMEM((VECS, 8192), BF16),
            pltpu.VMEM((32, VECS, 1024), F32),
        ],
        compiler_params=params(24),
        name="forward",
    )(near_count, near, mid, *vector_parts, u_factor, v_factor, first_blocks, second_blocks)

    sums = pl.pallas_call(
        share_sum_kernel,
        in_specs=[VMEM],
        out_specs=VMEM,
        out_shape=tall,
        compiler_params=params(8),
        name="share_sum",
    )(trade(shares.reshape(wide.shape), "cel", wide_groups))
    predicted, weighted = pl.pallas_call(
        weigh_kernel,
        in_specs=[VMEM] * 2,
        out_specs=[VMEM] * 2,
        out_shape=[jax.ShapeDtypeStruct((VECS, 1024), F32), tall],
        compiler_params=params(4),
        name="weigh",
    )(trade(sums, "cel", tall_groups), weights.reshape(-1, 128))

    copies = pl.pallas_call(
        copies_kernel,
        in_specs=[VMEM],
        out_specs=VMEM,
        out_shape=wide,
        compiler_params=params(8),
        name="copies",
    )(trade(weighted, "cel", tall_groups))
    data = trade(copies, "cel", wide_groups).reshape(32, VECS, 1024)

    lines = jax.ShapeDtypeStruct((8, 8192), BF16)
    kept, swapped = pl.pallas_call(
        adjoint_kernel,
        in_specs=[SMEM] * 3 + [VMEM] * 5,
        out_specs=[VMEM] * 2,
        out_shape=[jax.ShapeDtypeStruct(lines.shape, F32), lines],
        scratch_shapes=[pltpu.VMEM((VECS, 8192), F32)],
        compiler_params=params(24),
        name="adjoint",
    )(near_count, near, mid, data, u_factor, v_factor, first_blocks, second_blocks)
    pair = jax.ShapeDtypeStruct((2, 8192), BF16)
    terms = pl.pallas_call(
        chip_sum_kernel,
        in_specs=[VMEM] * 2,
        out_specs=[VMEM] * 4,
        out_shape=[jax.ShapeDtypeStruct(pair.shape, F32)] + [pair] * 3,
        compiler_params=params(4),
        name="chip_sum",
    )(kept, over_sta(swapped, 1))
    gradient = terms[0]
    for t in range(1, 4):
        gradient = gradient + over_sta(terms[t], 2 * t).astype(F32)
    return (predicted, gradient)


def solution(mesh):
    return jax.shard_map(
        body,
        mesh=mesh,
        in_specs=(
            P("sta", "cel"),
            P(None, "sta"),
            P(None, "cel"),
            P("sta"),
            P("sta", "cel", None, None),
            P("sta", None),
            P("sta", "cel", None, None),
            P("sta", "cel", None, None, None),
            P("sta", "cel", None, None, None),
        ),
        out_specs=(P(None, ("sta", "cel")), P("sta", "cel")),
        check_vma=False,
    )
```

profile of v0, /device:TPU:1, one launch (start us, length us, event | category | flops | bytes accessed | tf_op | source)
XLA Modules:
  0.0 104.1 jit_solution(15319836248038635833)
XLA Ops:
  0.6 3.3 %collective-permute-start = (bf16[2,8192]{1,0:T(2,128)(2,1)}, bf16[2,8192]{1,0:T(2,128)(2,1)S(1)}, u32[]{:S(2)}, u32[]{:S(2)}) collective-permute-start(bf16[2,8192]{1,0:T(2,128)(2,1)} %param.9), channel_id=1, source_target_pairs={{0,32},{32,0},{64,96},{96,64},{128,160},{160,128},{192,224},{224,1... | collective-permute-start | bytes 98312 | tf_op jit(solution)/shard_map/ppermute | solution.py:279
  4.0 0.0 copy-start.3
  4.0 0.7 copy-done.3
  4.6 0.0 copy-start.5
  4.6 0.7 copy-done.5
  5.3 0.0 copy-start.8
  5.3 1.0 copy-done.8
  6.3 0.0 copy-start.9
  6.3 0.9 copy-done.9
  7.2 0.0 copy-start.10
  7.2 3.4 %near_first.1 = (bf16[32,256,256]{2,1,0:T(8,128)(2,1)S(1)}, bf16[32,256,48]{2,1,0:T(8,128)(2,1)S(1)}, f32[3,32768]{1,0:T(4,128)S(1)}) custom-call(s32[1,32]{1,0:T(1,128)S(1)} %copy-done.5, s32[2,64]{1,0:T(2,128)S(1)} %bitcast.18, f32[3,32768]{1,0:T(4,128)S(1)} %copy-done.8, f32[3,8192]{1,0:T(4,128)S(1)} %copy-done.9), custom_call_target="tpu_custom_call" | custom-call | flops 402653184 | bytes 6291456 | tf_op jit(solution)/shard_map/near_first/pallas_call | solution.py:290
  10.7 0.0 collective-permute-done
  10.7 0.0 copy-done.10
  10.7 0.1 pad_maximum_fusion.refs_0_
  10.8 1.0 collective-permute-start.1
  11.8 1.6 %collective-permute-start.2 = (bf16[4,8192]{1,0:T(4,128)(2,1)S(1)}, bf16[4,8192]{1,0:T(4,128)(2,1)S(1)}, u32[]{:S(2)}, u32[]{:S(2)}) collective-permute-start(bf16[4,8192]{1,0:T(4,128)(2,1)S(1)} %pad_maximum_fusion.refs_0_), channel_id=1, source_target_pairs={{0,128},{32,160},{64,192},{96,224},{128,0},{160,32},{192,64},{224,... | collective-permute-start | bytes 196616 | tf_op jit(solution)/shard_map/ppermute | solution.py:279
  13.4 1.3 %collective-permute-start.3 = (bf16[4,8192]{1,0:T(4,128)(2,1)S(1)}, bf16[4,8192]{1,0:T(4,128)(2,1)S(1)}, u32[]{:S(2)}, u32[]{:S(2)}) collective-permute-start(bf16[4,8192]{1,0:T(4,128)(2,1)S(1)} %pad_maximum_fusion.refs_0_), channel_id=1, source_target_pairs={{0,192},{32,224},{64,128},{96,160},{128,64},{160,96},{192,0},{224,... | collective-permute-start | bytes 196616 | tf_op jit(solution)/shard_map/ppermute | solution.py:279
  14.8 0.0 copy-start.7
  14.8 0.6 near_second.1.refs_7_.second_blocks
  15.3 0.0 collective-permute-done.1.refs_1_
  15.4 2.0 %collective-permute-done.2.refs_2_ = bf16[4,8192]{1,0:T(4,128)(2,1)S(1)} collective-permute-done((bf16[4,8192]{1,0:T(4,128)(2,1)S(1)}, bf16[4,8192]{1,0:T(4,128)(2,1)S(1)}, u32[]{:S(2)}, u32[]{:S(2)}) %collective-permute-start.2) | collective-permute-done | bytes 65568 | tf_op jit(solution)/shard_map/ppermute | solution.py:279
  17.4 1.1 %collective-permute-done.3.refs_3_ = bf16[4,8192]{1,0:T(4,128)(2,1)S(1)} collective-permute-done((bf16[4,8192]{1,0:T(4,128)(2,1)S(1)}, bf16[4,8192]{1,0:T(4,128)(2,1)S(1)}, u32[]{:S(2)}, u32[]{:S(2)}) %collective-permute-start.3) | collective-permute-done | bytes 65568 | tf_op jit(solution)/shard_map/ppermute | solution.py:279
  18.5 0.0 copy-done
  18.5 0.0 copy-done.1
  18.5 0.0 copy-done.4
  18.5 0.0 copy-done.6
  18.5 0.0 copy-done.7
  18.5 4.4 %forward.1 = bf16[32,16,1024]{2,1,0:T(8,128)(2,1)S(1)} custom-call(s32[1,32]{1,0:T(1,128)S(1)} %copy-done.6, s32[2,64]{1,0:T(2,128)S(1)} %bitcast.20, s32[2,128]{1,0:T(2,128)S(1)} %bitcast.22, bf16[4,8192]{1,0:T(4,128)(2,1)S(1)} %pad_maximum_fusion.refs_0_, bf16[4,8192]{1,0:T(4,128)(2,1)S(1)} %collective-permute-done.1.refs_1_, ...), custom_call_target="tpu_custom_call" | custom-call | tf_op jit(solution)/shard_map/forward/pallas_call | solution.py:323
  22.9 0.0 copy-start.2
  22.9 18.4 %all_to_all.20.parts = bf16[8,4,16,1024]{3,2,1,0:T(8,128)(2,1)S(1)} all-to-all(bf16[8,4,16,1024]{3,2,1,0:T(8,128)(2,1)S(1)} %bitcast.16), channel_id=1, replica_groups={{0,1,2,3,4,5,6,7},{8,9,10,11,12,13,14,15},{16,17,18,19,20,21,22,23},{24..., dimensions={0} | all-to-all | bytes 2097152 | tf_op jit(solution)/shard_map/all_to_all | solution.py:285
  41.3 0.1 share_sum.1
  41.4 15.7 %all_to_all.21.parts = bf16[4,16,1024]{2,1,0:T(8,128)(2,1)S(1)} all-to-all(bf16[4,16,1024]{2,1,0:T(8,128)(2,1)S(1)} %share_sum.1), channel_id=1, replica_groups={{0,8,16,24},{1,9,17,25},{2,10,18,26},{3,11,19,27},{4,12,20,28},{5,13,21..., dimensions={0} | all-to-all | bytes 262144 | tf_op jit(solution)/shard_map/all_to_all | solution.py:285
  57.1 0.0 copy-done.2
  57.1 0.7 weigh.1
  57.8 9.6 %all_to_all.22.column = bf16[4,16,1024]{2,1,0:T(8,128)(2,1)S(1)} all-to-all(bf16[4,16,1024]{2,1,0:T(8,128)(2,1)S(1)} %get-tuple-element.21), channel_id=1, replica_groups={{0,8,16,24},{1,9,17,25},{2,10,18,26},{3,11,19,27},{4,12,20,28},{5,13,21..., dimensions={0} | all-to-all | bytes 262144 | tf_op jit(solution)/shard_map/all_to_all | solution.py:285
  67.4 0.1 copies.1
  67.5 14.4 %all_to_all.23 = bf16[8,4,16,1024]{3,2,1,0:T(8,128)(2,1)S(1)} all-to-all(bf16[8,4,16,1024]{3,2,1,0:T(8,128)(2,1)S(1)} %copies.1), channel_id=1, replica_groups={{0,1,2,3,4,5,6,7},{8,9,10,11,12,13,14,15},{16,17,18,19,20,21,22,23},{24..., dimensions={0} | all-to-all | bytes 2097152 | tf_op jit(solution)/shard_map/all_to_all | solution.py:285
  81.9 4.7 %adjoint.1 = (f32[8,8192]{1,0:T(8,128)S(1)}, bf16[8,8192]{1,0:T(8,128)(2,1)S(1)}) custom-call(s32[1,32]{1,0:T(1,128)S(1)} %copy-done.6, s32[2,64]{1,0:T(2,128)S(1)} %bitcast.21, s32[2,128]{1,0:T(2,128)S(1)} %bitcast.23, bf16[32,16,1024]{2,1,0:T(8,128)(2,1)S(1)} %bitcast.15, bf16[16,256,256]{2,1,0:T(8,128)(2,1)S(1)} %bitcast.12, ...), custom_call_target="tpu_custom_call" | custom-call | tf_op jit(solution)/shard_map/adjoint/pallas_call | solution.py:365
  86.6 7.5 %collective-permute-start.4 = (bf16[8,8192]{1,0:T(8,128)(2,1)S(1)}, bf16[8,8192]{1,0:T(8,128)(2,1)S(1)}, u32[]{:S(2)}, u32[]{:S(2)}) collective-permute-start(bf16[8,8192]{1,0:T(8,128)(2,1)S(1)} %get-tuple-element.23), channel_id=1, source_target_pairs={{0,32},{32,0},{64,96},{96,64},{128,160},{160,128},{192,224},{224,1... | collective-permute-start | bytes 393224 | tf_op jit(solution)/shard_map/ppermute | solution.py:279
  94.1 1.0 collective-permute-done.4.swapped
  95.1 0.1 chip_sum.1
  95.2 0.1 collective-permute-start.5
  95.3 4.2 %collective-permute-start.6 = (bf16[2,8192]{1,0:T(2,128)(2,1)S(1)}, bf16[2,8192]{1,0:T(2,128)(2,1)S(1)}, u32[]{:S(2)}, u32[]{:S(2)}) collective-permute-start(bf16[2,8192]{1,0:T(2,128)(2,1)S(1)} %get-tuple-element.26), channel_id=1, source_target_pairs={{0,128},{32,160},{64,192},{96,224},{128,0},{160,32},{192,64},{224,... | collective-permute-start | bytes 98312 | tf_op jit(solution)/shard_map/ppermute | solution.py:279
  99.4 0.0 collective-permute-start.7
  99.4 0.0 collective-permute-done.5
  99.4 1.6 %collective-permute-done.6 = bf16[2,8192]{1,0:T(2,128)(2,1)S(1)} collective-permute-done((bf16[2,8192]{1,0:T(2,128)(2,1)S(1)}, bf16[2,8192]{1,0:T(2,128)(2,1)S(1)}, u32[]{:S(2)}, u32[]{:S(2)}) %collective-permute-start.6) | collective-permute-done | bytes 32800 | tf_op jit(solution)/shard_map/ppermute | solution.py:279
  101.1 2.3 %collective-permute-done.7 = bf16[2,8192]{1,0:T(2,128)(2,1)S(1)} collective-permute-done((bf16[2,8192]{1,0:T(2,128)(2,1)S(1)}, bf16[2,8192]{1,0:T(2,128)(2,1)S(1)}, u32[]{:S(2)}, u32[]{:S(2)}) %collective-permute-start.7) | collective-permute-done | bytes 32800 | tf_op jit(solution)/shard_map/ppermute | solution.py:279
  103.4 0.7 convert_add_fusion
  (4 shorter events, 0.0 us)
Async XLA Ops:
  0.6 10.1 %collective-permute-start = (bf16[2,8192]{1,0:T(2,128)(2,1)}, bf16[2,8192]{1,0:T(2,128)(2,1)S(1)}, u32[]{:S(2)}, u32[]{:S(2)}) collective-permute-start(bf16[2,8192]{1,0:T(2,128)(2,1)} %param.9), channel_id=1, source_target_pairs={{0,32},{32,0},{64,96},{96,64},{128,160},{160,128},{192,224},{224,1... | collective-permute-start | bytes 98312 | tf_op jit(solution)/shard_map/ppermute | solution.py:279
  4.0 0.7 copy-start.3
  4.6 0.7 copy-start.5
  5.3 1.0 %copy-start.8 = (f32[3,32768]{1,0:T(4,128)S(1)}, f32[3,32768]{1,0:T(4,128)}, u32[]{:S(2)}) copy-start(f32[3,32768]{1,0:T(4,128)} %station_hbm.1) | copy-start | bytes 1179652
  6.3 0.9 copy-start.9
  7.2 3.5 %copy-start.10 = (bf16[2,8192]{1,0:T(2,128)(2,1)S(1)}, bf16[2,8192]{1,0:T(2,128)(2,1)}, u32[]{:S(2)}) copy-start(bf16[2,8192]{1,0:T(2,128)(2,1)} %param.9) | copy-start | bytes 98308
  10.8 4.6 %collective-permute-start.1 = (bf16[4,8192]{1,0:T(4,128)(2,1)S(1)}, bf16[4,8192]{1,0:T(4,128)(2,1)S(1)}, u32[]{:S(2)}, u32[]{:S(2)}) collective-permute-start(bf16[4,8192]{1,0:T(4,128)(2,1)S(1)} %pad_maximum_fusion.refs_0_), channel_id=1, source_target_pairs={{0,64},{32,96},{64,0},{96,32},{128,192},{160,224},{192,128},{224,1... | collective-permute-start | bytes 196616 | tf_op jit(solution)/shard_map/ppermute | solution.py:279
  11.8 5.6 %collective-permute-start.2 = (bf16[4,8192]{1,0:T(4,128)(2,1)S(1)}, bf16[4,8192]{1,0:T(4,128)(2,1)S(1)}, u32[]{:S(2)}, u32[]{:S(2)}) collective-permute-start(bf16[4,8192]{1,0:T(4,128)(2,1)S(1)} %pad_maximum_fusion.refs_0_), channel_id=1, source_target_pairs={{0,128},{32,160},{64,192},{96,224},{128,0},{160,32},{192,64},{224,... | collective-permute-start | bytes 196616 | tf_op jit(solution)/shard_map/ppermute | solution.py:279
  13.4 5.0 %collective-permute-start.3 = (bf16[4,8192]{1,0:T(4,128)(2,1)S(1)}, bf16[4,8192]{1,0:T(4,128)(2,1)S(1)}, u32[]{:S(2)}, u32[]{:S(2)}) collective-permute-start(bf16[4,8192]{1,0:T(4,128)(2,1)S(1)} %pad_maximum_fusion.refs_0_), channel_id=1, source_target_pairs={{0,192},{32,224},{64,128},{96,160},{128,64},{160,96},{192,0},{224,... | collective-permute-start | bytes 196616 | tf_op jit(solution)/shard_map/ppermute | solution.py:279
  14.7 3.7 %copy-start = (bf16[1,1,128,32,256]{4,3,2,1,0:T(8,128)(2,1)S(1)}, bf16[1,1,128,32,256]{4,3,2,1,0:T(8,128)(2,1)}, u32[]{:S(2)}) copy-start(bf16[1,1,128,32,256]{4,3,2,1,0:T(8,128)(2,1)} %param.16) | copy-start | bytes 6291460
  14.7 3.7 %copy-start.1 = (bf16[1,1,128,32,256]{4,3,2,1,0:T(8,128)(2,1)S(1)}, bf16[1,1,128,32,256]{4,3,2,1,0:T(8,128)(2,1)}, u32[]{:S(2)}) copy-start(bf16[1,1,128,32,256]{4,3,2,1,0:T(8,128)(2,1)} %param.17) | copy-start | bytes 6291460
  14.7 3.7 %copy-start.4 = (s32[1,1,64,2]{2,3,1,0:T(2,128)S(1)}, s32[1,1,64,2]{2,3,1,0:T(2,128)}, u32[]{:S(2)}) copy-start(s32[1,1,64,2]{2,3,1,0:T(2,128)} %param.13) | copy-start | bytes 1540
  14.7 3.7 %copy-start.6 = (s32[1,32]{1,0:T(1,128)S(1)}, s32[1,32]{1,0:T(1,128)}, u32[]{:S(2)}) copy-start(s32[1,32]{1,0:T(1,128)} %counts.7) | copy-start | bytes 388
  14.8 3.7 %copy-start.7 = (s32[1,1,128,2]{2,3,1,0:T(2,128)S(1)}, s32[1,1,128,2]{2,3,1,0:T(2,128)}, u32[]{:S(2)}) copy-start(s32[1,1,128,2]{2,3,1,0:T(2,128)} %param.15) | copy-start | bytes 3076
  22.9 34.2 %copy-start.2 = (f32[32768]{0:T(1024)S(1)}, f32[32768]{0:T(1024)}, u32[]{:S(2)}) copy-start(f32[32768]{0:T(1024)} %param.12) | copy-start | bytes 393220
  86.6 8.5 %collective-permute-start.4 = (bf16[8,8192]{1,0:T(8,128)(2,1)S(1)}, bf16[8,8192]{1,0:T(8,128)(2,1)S(1)}, u32[]{:S(2)}, u32[]{:S(2)}) collective-permute-start(bf16[8,8192]{1,0:T(8,128)(2,1)S(1)} %get-tuple-element.23), channel_id=1, source_target_pairs={{0,32},{32,0},{64,96},{96,64},{128,160},{160,128},{192,224},{224,1... | collective-permute-start | bytes 393224 | tf_op jit(solution)/shard_map/ppermute | solution.py:279
  95.2 4.3 %collective-permute-start.5 = (bf16[2,8192]{1,0:T(2,128)(2,1)S(1)}, bf16[2,8192]{1,0:T(2,128)(2,1)S(1)}, u32[]{:S(2)}, u32[]{:S(2)}) collective-permute-start(bf16[2,8192]{1,0:T(2,128)(2,1)S(1)} %get-tuple-element.25), channel_id=1, source_target_pairs={{0,64},{32,96},{64,0},{96,32},{128,192},{160,224},{192,128},{224,1... | collective-permute-start | bytes 98312 | tf_op jit(solution)/shard_map/ppermute | solution.py:279
  95.3 5.8 %collective-permute-start.6 = (bf16[2,8192]{1,0:T(2,128)(2,1)S(1)}, bf16[2,8192]{1,0:T(2,128)(2,1)S(1)}, u32[]{:S(2)}, u32[]{:S(2)}) collective-permute-start(bf16[2,8192]{1,0:T(2,128)(2,1)S(1)} %get-tuple-element.26), channel_id=1, source_target_pairs={{0,128},{32,160},{64,192},{96,224},{128,0},{160,32},{192,64},{224,... | collective-permute-start | bytes 98312 | tf_op jit(solution)/shard_map/ppermute | solution.py:279
  99.4 4.0 %collective-permute-start.7 = (bf16[2,8192]{1,0:T(2,128)(2,1)S(1)}, bf16[2,8192]{1,0:T(2,128)(2,1)S(1)}, u32[]{:S(2)}, u32[]{:S(2)}) collective-permute-start(bf16[2,8192]{1,0:T(2,128)(2,1)S(1)} %get-tuple-element.27), channel_id=1, source_target_pairs={{0,192},{32,224},{64,128},{96,160},{128,64},{160,96},{192,0},{224,... | collective-permute-start | bytes 98312 | tf_op jit(solution)/shard_map/ppermute | solution.py:279
where the time goes:
time: 105 us; the launch traced here: 104 us
  blocking collectives  58.1 us (55%)
  starting transfers between devices  19 us (18%)
  Pallas kernels  14.1 us (13%)
  waiting for transfers between devices  8.06 us (8%)
  local copies, waits for them, and re-layouts  3.31 us (3%)
    all_to_all x4, blocking collectives, trade(): return lax.all_to_all(x, axis, 0, 0, axis_index_groups=groups)  58.1 us
    ppermute x8, starting transfers between devices, over_sta(): return lax.ppermute(x, 'sta', [(i, i ^ k) for i in range(8)])  19 us
    ppermute x8, waiting for transfers between devices, over_sta(): return lax.ppermute(x, 'sta', [(i, i ^ k) for i in range(8)])  8.06 us
    pallas_call x1, Pallas kernels, body(): pl.pallas_call(adjoint_kernel, in_specs=[SMEM] * 3 + [VMEM] * 5, out_spec...  4.69 us
    pallas_call x1, Pallas kernels, body(): pl.pallas_call(forward_kernel, in_specs=[SMEM] * 3 + [VMEM] * 8, out_spec...  4.39 us
    pallas_call x1, Pallas kernels, body(): pl.pallas_call(near_first_kernel, in_specs=[SMEM] * 2 + [HBM] * 2, out_sp...  3.44 us
    unnamed x22, local copies, waits for them, and re-layouts  3.31 us
  transfers between devices with their start and end apart: 8, of which 5 were waited for; matrix products, arithmetic and copies ran while one was open for 0% of the time, Pallas kernels for 4%

commit v1 on v0

--- a/solution.py
+++ b/solution.py
@@ -186,30 +186,35 @@
 
 
 def share_sum_kernel(parts, out):
-    out[...] = sum_of(parts).astype(BF16)
+    total = sum_of(parts).astype(BF16)
+    for k in range(TALL):
+        out[k] = total
 
 
 def weigh_kernel(parts, weights, predicted, weighted):
     sta, cel = lax.axis_index("sta"), lax.axis_index("cel")
-    total = sum_of(parts)
-    share = weights[pl.ds(pl.multiple_of(cel * 8, 8), 8), :]
-    for r in range(8):
-        at = slice(r * 128, (r + 1) * 128)
-        value = (total[:, at] * share[r : r + 1, :]).astype(BF16)
-        for k in range(TALL):
-            weighted[k, :, at] = value
-    for place_of in range(8):
-
-        @pl.when(sta == place_of)
+    for h in range(TALL):
+        total = parts[0, h].astype(F32)
+        for k in range(1, TALL):
+            total = total + parts[k, h].astype(F32)
+
+        @pl.when(cel // WIDE == h)
         def _():
-            for k in range(8):
-                line = 2 * (k ^ place_of)
-                predicted[line : line + 2, :] = total[2 * k : 2 * k + 2]
-
-
-def copies_kernel(column, out):
-    for i in range(WIDE):
-        out[i] = column[...]
+            for place_of in range(8):
+
+                @pl.when(sta == place_of)
+                def _():
+                    for k in range(8):
+                        line = 2 * (k ^ place_of)
+                        predicted[line : line + 2, :] = total[2 * k : 2 * k + 2]
+
+        share = h * WIDE + cel % WIDE
+        scale = weights[pl.ds(pl.multiple_of(share * 8, 8), 8), :]
+        for r in range(8):
+            at = slice(r * 128, (r + 1) * 128)
+            value = (total[:, at] * scale[r : r + 1, :]).astype(BF16)
+            for i in range(WIDE):
+                weighted[i, h, :, at] = value
 
 
 def adjoint_kernel(
@@ -287,6 +292,7 @@
     half = HALF * GROUP
     cell_tiles = cell_xyz.shape[1] // TILE
     other_vectors = over_sta(model_vectors, 1)
+    inputs = (near_count, near, station_xyz, cell_xyz)
     first_blocks, features, stations = pl.pallas_call(
         near_first_kernel,
         in_specs=[SMEM] * 2 + [HBM] * 2,
@@ -302,7 +308,7 @@
             flops=half * 2 * 512 * 48 * 256, bytes_accessed=6 * MIB, transcendentals=half * 65536
         ),
         name="near_first",
-    )(near_count, near, station_xyz, cell_xyz)
+    )(*[pltpu.with_memory_space_constraint(a, pltpu.HBM) for a in inputs])
     other_vectors, features = lax.optimization_barrier((other_vectors, features))
     chip_vectors = jnp.concatenate((model_vectors, other_vectors), axis=0)
     vector_parts = [chip_vectors] + [over_sta(chip_vectors, 2 * k) for k in range(1, 4)]
@@ -338,7 +344,7 @@
         share_sum_kernel,
         in_specs=[VMEM],
         out_specs=VMEM,
-        out_shape=tall,
+        out_shape=jax.ShapeDtypeStruct((TALL, *tall.shape), BF16),
         compiler_params=params(8),
         name="share_sum",
     )(trade(shares.reshape(wide.shape), "cel", wide_groups))
@@ -346,20 +352,11 @@
         weigh_kernel,
         in_specs=[VMEM] * 2,
         out_specs=[VMEM] * 2,
-        out_shape=[jax.ShapeDtypeStruct((VECS, 1024), F32), tall],
-        compiler_params=params(4),
+        out_shape=[jax.ShapeDtypeStruct((VECS, 1024), F32), wide],
+        compiler_params=params(8),
         name="weigh",
     )(trade(sums, "cel", tall_groups), weights.reshape(-1, 128))
-
-    copies = pl.pallas_call(
-        copies_kernel,
-        in_specs=[VMEM],
-        out_specs=VMEM,
-        out_shape=wide,
-        compiler_params=params(8),
-        name="copies",
-    )(trade(weighted, "cel", tall_groups))
-    data = trade(copies, "cel", wide_groups).reshape(32, VECS, 1024)
+    data = trade(weighted, "cel", wide_groups).reshape(32, VECS, 1024)
 
     lines = jax.ShapeDtypeStruct((8, 8192), BF16)
     kept, swapped = pl.pallas_call(

time: 105 us -> 101 us (0.962)
  local copies, waits for them, and re-layouts: 3.31 us -> 0.03 us
  waiting for transfers between devices: 8.06 us -> 6.01 us
    unnamed x22 -> x14, local copies, waits for them, and re-layouts: 3.31 us -> 0.03 us
    ppermute x8, waiting for transfers between devices: 8.06 us -> 6.01 us  [over_sta(): return lax.ppermute(x, 'sta', [(i, i ^ k) for i in range(8)])]
    all_to_all x4 -> x3, blocking collectives: 58.1 us -> 58.2 us  [trade(): return lax.all_to_all(x, axis, 0, 0, axis_index_groups=groups)]
  transfers between devices with their start and end apart: 8 -> 8, of which waited for: 5 -> 5; matrix products, arithmetic and copies ran while one was open for 0% -> 0% of each run, Pallas kernels for 4% -> 5%
where the time goes in v1:
time: 101 us; the launch traced here: 99.2 us
  blocking collectives  58.2 us (58%)
  starting transfers between devices  18.3 us (18%)
  Pallas kernels  15 us (15%)
  waiting for transfers between devices  6.01 us (6%)
    all_to_all x3, blocking collectives, trade(): return lax.all_to_all(x, axis, 0, 0, axis_index_groups=groups)  58.2 us
    ppermute x8, starting transfers between devices, over_sta(): return lax.ppermute(x, 'sta', [(i, i ^ k) for i in range(8)])  18.3 us
    ppermute x8, waiting for transfers between devices, over_sta(): return lax.ppermute(x, 'sta', [(i, i ^ k) for i in range(8)])  6.01 us
    pallas_call x1, Pallas kernels, body(): pl.pallas_call(adjoint_kernel, in_specs=[SMEM] * 3 + [VMEM] * 5, out_spec...  4.69 us
    pallas_call x1, Pallas kernels, body(): pl.pallas_call(forward_kernel, in_specs=[SMEM] * 3 + [VMEM] * 8, out_spec...  4.39 us
    pallas_call x1, Pallas kernels, body(): pl.pallas_call(near_first_kernel, in_specs=[SMEM] * 2 + [HBM] * 2, out_sp...  4.29 us
  transfers between devices with their start and end apart: 8, of which 5 were waited for; matrix products, arithmetic and copies ran while one was open for 0% of the time, Pallas kernels for 5%

profile of v1, /device:TPU:1, one launch (start us, length us, event | category | flops | bytes accessed | tf_op | source)
XLA Modules:
  0.0 99.2 jit_solution(2359452270695465921)
XLA Ops:
  0.6 0.0 copy-start.6
  0.6 0.0 copy-start.3
  0.7 0.0 copy-start.4
  0.7 3.3 %collective-permute-start = (bf16[2,8192]{1,0:T(2,128)(2,1)}, bf16[2,8192]{1,0:T(2,128)(2,1)S(1)}, u32[]{:S(2)}, u32[]{:S(2)}) collective-permute-start(bf16[2,8192]{1,0:T(2,128)(2,1)} %param.9), channel_id=1, source_target_pairs={{0,32},{32,0},{64,96},{96,64},{128,160},{160,128},{192,224},{224,1... | collective-permute-start | bytes 98312 | tf_op jit(solution)/shard_map/ppermute | solution.py:284
  4.0 4.3 %near_first.1 = (bf16[32,256,256]{2,1,0:T(8,128)(2,1)S(1)}, bf16[32,256,48]{2,1,0:T(8,128)(2,1)S(1)}, f32[3,32768]{1,0:T(4,128)S(1)}) custom-call(s32[1,32]{1,0:T(1,128)} %counts.7, s32[2,64]{1,0:T(2,128)} %bitcast.18, f32[3,32768]{1,0:T(4,128)} %station_hbm.1, f32[3,8192]{1,0:T(4,128)} %cell_hbm.1), custom_call_target="tpu_custom_call" | custom-call | flops 402653184 | bytes 6291456 | tf_op jit(solution)/shard_map/near_first/pallas_call | solution.py:296
  8.3 0.0 collective-permute-done
  8.3 0.0 copy-done.6
  8.3 0.1 pad_maximum_fusion.refs_0_
  8.4 0.1 collective-permute-start.1
  8.5 2.5 %collective-permute-start.2 = (bf16[4,8192]{1,0:T(4,128)(2,1)S(1)}, bf16[4,8192]{1,0:T(4,128)(2,1)S(1)}, u32[]{:S(2)}, u32[]{:S(2)}) collective-permute-start(bf16[4,8192]{1,0:T(4,128)(2,1)S(1)} %pad_maximum_fusion.refs_0_), channel_id=1, source_target_pairs={{0,128},{32,160},{64,192},{96,224},{128,0},{160,32},{192,64},{224,... | collective-permute-start | bytes 196616 | tf_op jit(solution)/shard_map/ppermute | solution.py:284
  11.0 1.3 %collective-permute-start.3 = (bf16[4,8192]{1,0:T(4,128)(2,1)S(1)}, bf16[4,8192]{1,0:T(4,128)(2,1)S(1)}, u32[]{:S(2)}, u32[]{:S(2)}) collective-permute-start(bf16[4,8192]{1,0:T(4,128)(2,1)S(1)} %pad_maximum_fusion.refs_0_), channel_id=1, source_target_pairs={{0,192},{32,224},{64,128},{96,160},{128,64},{160,96},{192,0},{224,... | collective-permute-start | bytes 196616 | tf_op jit(solution)/shard_map/ppermute | solution.py:284
  12.3 0.0 copy-done.3
  12.3 0.0 copy-done.4
  12.3 0.0 copy-start
  12.3 0.0 copy-start.1
  12.3 0.0 copy-start.5
  12.4 0.6 near_second.1.refs_7_.second_blocks
  12.9 0.0 collective-permute-done.1.refs_1_
  13.0 1.0 %collective-permute-done.2.refs_2_ = bf16[4,8192]{1,0:T(4,128)(2,1)S(1)} collective-permute-done((bf16[4,8192]{1,0:T(4,128)(2,1)S(1)}, bf16[4,8192]{1,0:T(4,128)(2,1)S(1)}, u32[]{:S(2)}, u32[]{:S(2)}) %collective-permute-start.2) | collective-permute-done | bytes 65568 | tf_op jit(solution)/shard_map/ppermute | solution.py:284
  14.0 1.9 %collective-permute-done.3.refs_3_ = bf16[4,8192]{1,0:T(4,128)(2,1)S(1)} collective-permute-done((bf16[4,8192]{1,0:T(4,128)(2,1)S(1)}, bf16[4,8192]{1,0:T(4,128)(2,1)S(1)}, u32[]{:S(2)}, u32[]{:S(2)}) %collective-permute-start.3) | collective-permute-done | bytes 65568 | tf_op jit(solution)/shard_map/ppermute | solution.py:284
  15.8 0.0 copy-done
  15.8 0.0 copy-done.1
  15.8 0.0 copy-done.5
  15.9 4.4 %forward.1 = bf16[32,16,1024]{2,1,0:T(8,128)(2,1)S(1)} custom-call(s32[1,32]{1,0:T(1,128)S(1)} %copy-done.4, s32[2,64]{1,0:T(2,128)S(1)} %bitcast.20, s32[2,128]{1,0:T(2,128)S(1)} %bitcast.22, bf16[4,8192]{1,0:T(4,128)(2,1)S(1)} %pad_maximum_fusion.refs_0_, bf16[4,8192]{1,0:T(4,128)(2,1)S(1)} %collective-permute-done.1.refs_1_, ...), custom_call_target="tpu_custom_call" | custom-call | tf_op jit(solution)/shard_map/forward/pallas_call | solution.py:329
  20.3 0.0 copy-start.2
  20.3 17.3 %all_to_all.15.parts = bf16[8,4,16,1024]{3,2,1,0:T(8,128)(2,1)S(1)} all-to-all(bf16[8,4,16,1024]{3,2,1,0:T(8,128)(2,1)S(1)} %bitcast.16), channel_id=1, replica_groups={{0,1,2,3,4,5,6,7},{8,9,10,11,12,13,14,15},{16,17,18,19,20,21,22,23},{24..., dimensions={0} | all-to-all | bytes 2097152 | tf_op jit(solution)/shard_map/all_to_all | solution.py:290
  37.6 0.1 share_sum.1
  37.7 21.4 %all_to_all.16.parts = bf16[4,4,16,1024]{3,2,1,0:T(8,128)(2,1)S(1)} all-to-all(bf16[4,4,16,1024]{3,2,1,0:T(8,128)(2,1)S(1)} %share_sum.1), channel_id=1, replica_groups={{0,8,16,24},{1,9,17,25},{2,10,18,26},{3,11,19,27},{4,12,20,28},{5,13,21..., dimensions={0} | all-to-all | bytes 1048576 | tf_op jit(solution)/shard_map/all_to_all | solution.py:290
  59.2 0.0 copy-done.2
  59.2 0.9 weigh.1
  60.1 19.5 %all_to_all.17 = bf16[8,4,16,1024]{3,2,1,0:T(8,128)(2,1)S(1)} all-to-all(bf16[8,4,16,1024]{3,2,1,0:T(8,128)(2,1)S(1)} %get-tuple-element.21), channel_id=1, replica_groups={{0,1,2,3,4,5,6,7},{8,9,10,11,12,13,14,15},{16,17,18,19,20,21,22,23},{24..., dimensions={0} | all-to-all | bytes 2097152 | tf_op jit(solution)/shard_map/all_to_all | solution.py:290
  79.5 4.7 %adjoint.1 = (f32[8,8192]{1,0:T(8,128)S(1)}, bf16[8,8192]{1,0:T(8,128)(2,1)S(1)}) custom-call(s32[1,32]{1,0:T(1,128)S(1)} %copy-done.4, s32[2,64]{1,0:T(2,128)S(1)} %bitcast.21, s32[2,128]{1,0:T(2,128)S(1)} %bitcast.23, bf16[32,16,1024]{2,1,0:T(8,128)(2,1)S(1)} %bitcast.15, bf16[16,256,256]{2,1,0:T(8,128)(2,1)S(1)} %bitcast.12, ...), custom_call_target="tpu_custom_call" | custom-call | tf_op jit(solution)/shard_map/adjoint/pallas_call | solution.py:362
  84.2 3.2 %collective-permute-start.4 = (bf16[8,8192]{1,0:T(8,128)(2,1)S(1)}, bf16[8,8192]{1,0:T(8,128)(2,1)S(1)}, u32[]{:S(2)}, u32[]{:S(2)}) collective-permute-start(bf16[8,8192]{1,0:T(8,128)(2,1)S(1)} %get-tuple-element.23), channel_id=1, source_target_pairs={{0,32},{32,0},{64,96},{96,64},{128,160},{160,128},{192,224},{224,1... | collective-permute-start | bytes 393224 | tf_op jit(solution)/shard_map/ppermute | solution.py:284
  87.4 1.0 collective-permute-done.4.swapped
  88.4 0.1 chip_sum.1
  88.5 5.4 %collective-permute-start.5 = (bf16[2,8192]{1,0:T(2,128)(2,1)S(1)}, bf16[2,8192]{1,0:T(2,128)(2,1)S(1)}, u32[]{:S(2)}, u32[]{:S(2)}) collective-permute-start(bf16[2,8192]{1,0:T(2,128)(2,1)S(1)} %get-tuple-element.25), channel_id=1, source_target_pairs={{0,64},{32,96},{64,0},{96,32},{128,192},{160,224},{192,128},{224,1... | collective-permute-start | bytes 98312 | tf_op jit(solution)/shard_map/ppermute | solution.py:284
  93.8 0.3 collective-permute-start.6
  94.2 2.2 %collective-permute-start.7 = (bf16[2,8192]{1,0:T(2,128)(2,1)S(1)}, bf16[2,8192]{1,0:T(2,128)(2,1)S(1)}, u32[]{:S(2)}, u32[]{:S(2)}) collective-permute-start(bf16[2,8192]{1,0:T(2,128)(2,1)S(1)} %get-tuple-element.27), channel_id=1, source_target_pairs={{0,192},{32,224},{64,128},{96,160},{128,64},{160,96},{192,0},{224,... | collective-permute-start | bytes 98312 | tf_op jit(solution)/shard_map/ppermute | solution.py:284
  96.3 0.0 collective-permute-done.5
  96.3 1.8 %collective-permute-done.6 = bf16[2,8192]{1,0:T(2,128)(2,1)S(1)} collective-permute-done((bf16[2,8192]{1,0:T(2,128)(2,1)S(1)}, bf16[2,8192]{1,0:T(2,128)(2,1)S(1)}, u32[]{:S(2)}, u32[]{:S(2)}) %collective-permute-start.6) | collective-permute-done | bytes 32800 | tf_op jit(solution)/shard_map/ppermute | solution.py:284
  98.1 0.3 collective-permute-done.7
  98.5 0.7 convert_add_fusion
Async XLA Ops:
  0.6 7.7 %copy-start.6 = (bf16[2,8192]{1,0:T(2,128)(2,1)S(1)}, bf16[2,8192]{1,0:T(2,128)(2,1)}, u32[]{:S(2)}) copy-start(bf16[2,8192]{1,0:T(2,128)(2,1)} %param.9) | copy-start | bytes 98308
  0.6 11.7 %copy-start.3 = (s32[1,1,64,2]{2,3,1,0:T(2,128)S(1)}, s32[1,1,64,2]{2,3,1,0:T(2,128)}, u32[]{:S(2)}) copy-start(s32[1,1,64,2]{2,3,1,0:T(2,128)} %param.13) | copy-start | bytes 1540
  0.7 11.7 %copy-start.4 = (s32[1,32]{1,0:T(1,128)S(1)}, s32[1,32]{1,0:T(1,128)}, u32[]{:S(2)}) copy-start(s32[1,32]{1,0:T(1,128)} %counts.7) | copy-start | bytes 388
  0.7 7.6 %collective-permute-start = (bf16[2,8192]{1,0:T(2,128)(2,1)}, bf16[2,8192]{1,0:T(2,128)(2,1)S(1)}, u32[]{:S(2)}, u32[]{:S(2)}) collective-permute-start(bf16[2,8192]{1,0:T(2,128)(2,1)} %param.9), channel_id=1, source_target_pairs={{0,32},{32,0},{64,96},{96,64},{128,160},{160,128},{192,224},{224,1... | collective-permute-start | bytes 98312 | tf_op jit(solution)/shard_map/ppermute | solution.py:284
  8.4 4.6 %collective-permute-start.1 = (bf16[4,8192]{1,0:T(4,128)(2,1)S(1)}, bf16[4,8192]{1,0:T(4,128)(2,1)S(1)}, u32[]{:S(2)}, u32[]{:S(2)}) collective-permute-start(bf16[4,8192]{1,0:T(4,128)(2,1)S(1)} %pad_maximum_fusion.refs_0_), channel_id=1, source_target_pairs={{0,64},{32,96},{64,0},{96,32},{128,192},{160,224},{192,128},{224,1... | collective-permute-start | bytes 196616 | tf_op jit(solution)/shard_map/ppermute | solution.py:284
  8.5 5.5 %collective-permute-start.2 = (bf16[4,8192]{1,0:T(4,128)(2,1)S(1)}, bf16[4,8192]{1,0:T(4,128)(2,1)S(1)}, u32[]{:S(2)}, u32[]{:S(2)}) collective-permute-start(bf16[4,8192]{1,0:T(4,128)(2,1)S(1)} %pad_maximum_fusion.refs_0_), channel_id=1, source_target_pairs={{0,128},{32,160},{64,192},{96,224},{128,0},{160,32},{192,64},{224,... | collective-permute-start | bytes 196616 | tf_op jit(solution)/shard_map/ppermute | solution.py:284
  11.0 4.8 %collective-permute-start.3 = (bf16[4,8192]{1,0:T(4,128)(2,1)S(1)}, bf16[4,8192]{1,0:T(4,128)(2,1)S(1)}, u32[]{:S(2)}, u32[]{:S(2)}) collective-permute-start(bf16[4,8192]{1,0:T(4,128)(2,1)S(1)} %pad_maximum_fusion.refs_0_), channel_id=1, source_target_pairs={{0,192},{32,224},{64,128},{96,160},{128,64},{160,96},{192,0},{224,... | collective-permute-start | bytes 196616 | tf_op jit(solution)/shard_map/ppermute | solution.py:284
  12.3 3.5 %copy-start = (bf16[1,1,128,32,256]{4,3,2,1,0:T(8,128)(2,1)S(1)}, bf16[1,1,128,32,256]{4,3,2,1,0:T(8,128)(2,1)}, u32[]{:S(2)}) copy-start(bf16[1,1,128,32,256]{4,3,2,1,0:T(8,128)(2,1)} %param.16) | copy-start | bytes 6291460
  12.3 3.5 %copy-start.1 = (bf16[1,1,128,32,256]{4,3,2,1,0:T(8,128)(2,1)S(1)}, bf16[1,1,128,32,256]{4,3,2,1,0:T(8,128)(2,1)}, u32[]{:S(2)}) copy-start(bf16[1,1,128,32,256]{4,3,2,1,0:T(8,128)(2,1)} %param.17) | copy-start | bytes 6291460
  12.3 3.5 %copy-start.5 = (s32[1,1,128,2]{2,3,1,0:T(2,128)S(1)}, s32[1,1,128,2]{2,3,1,0:T(2,128)}, u32[]{:S(2)}) copy-start(s32[1,1,128,2]{2,3,1,0:T(2,128)} %param.15) | copy-start | bytes 3076
  20.3 38.9 %copy-start.2 = (f32[32768]{0:T(1024)S(1)}, f32[32768]{0:T(1024)}, u32[]{:S(2)}) copy-start(f32[32768]{0:T(1024)} %param.12) | copy-start | bytes 393220
  84.2 4.2 %collective-permute-start.4 = (bf16[8,8192]{1,0:T(8,128)(2,1)S(1)}, bf16[8,8192]{1,0:T(8,128)(2,1)S(1)}, u32[]{:S(2)}, u32[]{:S(2)}) collective-permute-start(bf16[8,8192]{1,0:T(8,128)(2,1)S(1)} %get-tuple-element.23), channel_id=1, source_target_pairs={{0,32},{32,0},{64,96},{96,64},{128,160},{160,128},{192,224},{224,1... | collective-permute-start | bytes 393224 | tf_op jit(solution)/shard_map/ppermute | solution.py:284
  88.5 7.9 %collective-permute-start.5 = (bf16[2,8192]{1,0:T(2,128)(2,1)S(1)}, bf16[2,8192]{1,0:T(2,128)(2,1)S(1)}, u32[]{:S(2)}, u32[]{:S(2)}) collective-permute-start(bf16[2,8192]{1,0:T(2,128)(2,1)S(1)} %get-tuple-element.25), channel_id=1, source_target_pairs={{0,64},{32,96},{64,0},{96,32},{128,192},{160,224},{192,128},{224,1... | collective-permute-start | bytes 98312 | tf_op jit(solution)/shard_map/ppermute | solution.py:284
  93.8 4.3 %collective-permute-start.6 = (bf16[2,8192]{1,0:T(2,128)(2,1)S(1)}, bf16[2,8192]{1,0:T(2,128)(2,1)S(1)}, u32[]{:S(2)}, u32[]{:S(2)}) collective-permute-start(bf16[2,8192]{1,0:T(2,128)(2,1)S(1)} %get-tuple-element.26), channel_id=1, source_target_pairs={{0,128},{32,160},{64,192},{96,224},{128,0},{160,32},{192,64},{224,... | collective-permute-start | bytes 98312 | tf_op jit(solution)/shard_map/ppermute | solution.py:284
  94.2 4.3 %collective-permute-start.7 = (bf16[2,8192]{1,0:T(2,128)(2,1)S(1)}, bf16[2,8192]{1,0:T(2,128)(2,1)S(1)}, u32[]{:S(2)}, u32[]{:S(2)}) collective-permute-start(bf16[2,8192]{1,0:T(2,128)(2,1)S(1)} %get-tuple-element.27), channel_id=1, source_target_pairs={{0,192},{32,224},{64,128},{96,160},{128,64},{160,96},{192,0},{224,... | collective-permute-start | bytes 98312 | tf_op jit(solution)/shard_map/ppermute | solution.py:284

commit v2 on v1

--- a/solution.py
+++ b/solution.py
@@ -9,7 +9,8 @@
 
 VOLUME = 0.03125
 FIELD = (0.17101, 0.46985, -0.86603)
-ROOT = (3.0 * VOLUME) ** 0.5
+SHRINK = VOLUME ** (-1.0 / 3.0)
+SLOPE = 3.0**0.5
 
 TILE = 256
 VECS = 16
@@ -41,14 +42,14 @@
 
 
 def field_of(x, y, z):
-    return ROOT * (FIELD[0] * x + FIELD[1] * y + FIELD[2] * z)
+    return SLOPE * (FIELD[0] * x + FIELD[1] * y + FIELD[2] * z)
 
 
 def near_group(g, pairs, stations, features, out, first):
     lines = lax.broadcasted_iota(jnp.int32, (8, TILE), 0)
     for j in range(GROUP):
         at = lanes_of(pairs[0, g * GROUP + j])
-        x, y, z = (stations[d : d + 1, at] for d in range(3))
+        x, y, z = (SHRINK * stations[d : d + 1, at] for d in range(3))
         one = jnp.ones_like(x)
         wide = stack(lines, ((0, x), (1, y), (2, z), (3, x * x + y * y + z * z), (5, one)))
         flat = stack(lines, ((3, field_of(x, y, z)), (6, one)))
@@ -62,9 +63,8 @@
         inverse = lax.rsqrt(product(wide))
         along = product(flat)
         square = inverse * inverse
-        out[(g - first) * GROUP + j] = (
-            (along * along * square - VOLUME) * (square * inverse)
-        ).astype(BF16)
+        along = along * square
+        out[(g - first) * GROUP + j] = ((along * along - square) * inverse).astype(BF16)
 
 
 def near_first_kernel(counts, pairs, station_hbm, cell_hbm, out, features, stations, cells, sem):
@@ -80,7 +80,7 @@
         lines = lax.broadcasted_iota(jnp.int32, (8, TILE), 0)
         for q in range(4):
             at = lanes_of(i * 4 + q)
-            x, y, z = (cells[d : d + 1, at] for d in range(3))
+            x, y, z = (SHRINK * cells[d : d + 1, at] for d in range(3))
             square = x * x + y * y + z * z
             block = stack(
                 lines,
@@ -139,10 +139,10 @@
 
 
 def forward_kernel(counts, near, mid, *refs):
-    parts = refs[:4]
-    u_ref, v_ref, first_blocks, second_blocks, out, stacked, vectors, total = refs[4:]
-    for k in range(4):
-        stacked[4 * k : 4 * k + 4, :] = parts[k][...].astype(F32)
+    parts = refs[:8]
+    u_ref, v_ref, first_blocks, second_blocks, out, stacked, vectors, total = refs[8:]
+    for k in range(8):
+        stacked[2 * k : 2 * k + 2, :] = parts[k][...].astype(F32)
     vectors[...] = stacked[...].astype(BF16)
     total[...] = jnp.zeros_like(total)
     mask = block_mask()
@@ -186,17 +186,14 @@
 
 
 def share_sum_kernel(parts, out):
-    total = sum_of(parts).astype(BF16)
-    for k in range(TALL):
-        out[k] = total
-
-
-def weigh_kernel(parts, weights, predicted, weighted):
+    out[...] = sum_of(parts).astype(BF16)
+
+
+def weigh_kernel(own, one, two, three, weights, predicted, weighted):
     sta, cel = lax.axis_index("sta"), lax.axis_index("cel")
     for h in range(TALL):
-        total = parts[0, h].astype(F32)
-        for k in range(1, TALL):
-            total = total + parts[k, h].astype(F32)
+        total = own[h].astype(F32) + one[h].astype(F32)
+        total = total + (two[h].astype(F32) + three[h].astype(F32))
 
         @pl.when(cel // WIDE == h)
         def _():
@@ -284,14 +281,16 @@
         return lax.ppermute(x, "sta", [(i, i ^ k) for i in range(8)])
 
     wide_groups = [[WIDE * h + w for w in range(WIDE)] for h in range(TALL)]
-    tall_groups = [[WIDE * h + w for h in range(TALL)] for w in range(WIDE)]
+
+    def over_tall(x, k):
+        return lax.ppermute(x, "cel", [(i, i ^ (WIDE * k)) for i in range(32)])
 
     def trade(x, axis, groups):
         return lax.all_to_all(x, axis, 0, 0, axis_index_groups=groups)
 
     half = HALF * GROUP
     cell_tiles = cell_xyz.shape[1] // TILE
-    other_vectors = over_sta(model_vectors, 1)
+    same_core = [over_sta(model_vectors, 2 * k) for k in range(1, 4)]
     inputs = (near_count, near, station_xyz, cell_xyz)
     first_blocks, features, stations = pl.pallas_call(
         near_first_kernel,
@@ -309,9 +308,10 @@
         ),
         name="near_first",
     )(*[pltpu.with_memory_space_constraint(a, pltpu.HBM) for a in inputs])
-    other_vectors, features = lax.optimization_barrier((other_vectors, features))
-    chip_vectors = jnp.concatenate((model_vectors, other_vectors), axis=0)
-    vector_parts = [chip_vectors] + [over_sta(chip_vectors, 2 * k) for k in range(1, 4)]
+    same_core, features = lax.optimization_barrier((same_core, features))
+    vector_parts = []
+    for vectors in [model_vectors] + same_core:
+        vector_parts += [vectors, over_sta(vectors, 1)]
     second_blocks = pl.pallas_call(
         near_second_kernel,
         in_specs=[SMEM] * 2 + [VMEM] * 2,
@@ -328,7 +328,7 @@
     tall = jax.ShapeDtypeStruct((TALL, VECS, 1024), BF16)
     shares = pl.pallas_call(
         forward_kernel,
-        in_specs=[SMEM] * 3 + [VMEM] * 8,
+        in_specs=[SMEM] * 3 + [VMEM] * 12,
         out_specs=VMEM,
         out_shape=jax.ShapeDtypeStruct((32, VECS, 1024), BF16),
         scratch_shapes=[
@@ -344,18 +344,18 @@
         share_sum_kernel,
         in_specs=[VMEM],
         out_specs=VMEM,
-        out_shape=jax.ShapeDtypeStruct((TALL, *tall.shape), BF16),
+        out_shape=tall,
         compiler_params=params(8),
         name="share_sum",
     )(trade(shares.reshape(wide.shape), "cel", wide_groups))
     predicted, weighted = pl.pallas_call(
         weigh_kernel,
-        in_specs=[VMEM] * 2,
+        in_specs=[VMEM] * 5,
         out_specs=[VMEM] * 2,
         out_shape=[jax.ShapeDtypeStruct((VECS, 1024), F32), wide],
         compiler_params=params(8),
         name="weigh",
-    )(trade(sums, "cel", tall_groups), weights.reshape(-1, 128))
+    )(sums, *[over_tall(sums, k) for k in range(1, TALL)], weights.reshape(-1, 128))
     data = trade(weighted, "cel", wide_groups).reshape(32, VECS, 1024)
 
     lines = jax.ShapeDtypeStruct((8, 8192), BF16)

time: 101 us -> 99.3 us (0.983); the launches traced: 99.2 us -> 99.4 us
  blocking collectives: 58.2 us -> 38.5 us
  waiting for transfers between devices: 6.01 us -> 16.7 us
  starting transfers between devices: 18.3 us -> 27.6 us
  local copies, waits for them, and re-layouts: 0.03 us -> 1.4 us
  Pallas kernels: 15 us -> 13.8 us
    all_to_all x3 -> x2, blocking collectives: 58.2 us -> 38.5 us  [trade(): return lax.all_to_all(x, axis, 0, 0, axis_index_groups=groups)]
    ppermute x0 -> x3, waiting for transfers between devices: none -> 11.5 us  [over_tall(): return lax.ppermute(x, 'cel', [(i, i ^ WIDE * k) for i in range(32)])]
    ppermute x0 -> x3, starting transfers between devices: none -> 8.25 us  [over_tall(): return lax.ppermute(x, 'cel', [(i, i ^ WIDE * k) for i in range(32)])]
    unnamed x14, local copies, waits for them, and re-layouts: 0.03 us -> 1.4 us
    ppermute x8 -> x11, starting transfers between devices: 18.3 us -> 19.3 us  [over_sta(): return lax.ppermute(x, 'sta', [(i, i ^ k) for i in range(8)])]
    ppermute x8 -> x11, waiting for transfers between devices: 6.01 us -> 5.19 us  [over_sta(): return lax.ppermute(x, 'sta', [(i, i ^ k) for i in range(8)])]
  transfers between devices with their start and end apart: 8 -> 14, of which waited for: 5 -> 8; matrix products, arithmetic and copies ran while one was open for 0% -> 0% of each run, Pallas kernels for 5% -> 4%
where the time goes in v2:
time: 99.3 us; the launch traced here: 99.4 us
  blocking collectives  38.5 us (39%)
  starting transfers between devices  27.6 us (28%)
  waiting for transfers between devices  16.7 us (17%)
  Pallas kernels  13.8 us (14%)
  local copies, waits for them, and re-layouts  1.4 us (1%)
    all_to_all x2, blocking collectives, trade(): return lax.all_to_all(x, axis, 0, 0, axis_index_groups=groups)  38.5 us
    ppermute x11, starting transfers between devices, over_sta(): return lax.ppermute(x, 'sta', [(i, i ^ k) for i in range(8)])  19.3 us
    ppermute x3, waiting for transfers between devices, over_tall(): return lax.ppermute(x, 'cel', [(i, i ^ WIDE * k) for i in range(32)])  11.5 us
    ppermute x3, starting transfers between devices, over_tall(): return lax.ppermute(x, 'cel', [(i, i ^ WIDE * k) for i in range(32)])  8.25 us
    ppermute x11, waiting for transfers between devices, over_sta(): return lax.ppermute(x, 'sta', [(i, i ^ k) for i in range(8)])  5.19 us
    pallas_call x1, Pallas kernels, body(): pl.pallas_call(adjoint_kernel, in_specs=[SMEM] * 3 + [VMEM] * 5, out_spec...  4.3 us
    pallas_call x1, Pallas kernels, body(): pl.pallas_call(forward_kernel, in_specs=[SMEM] * 3 + [VMEM] * 12, out_spe...  4.22 us
    pallas_call x1, Pallas kernels, body(): pl.pallas_call(near_first_kernel, in_specs=[SMEM] * 2 + [HBM] * 2, out_sp...  3.59 us
  transfers between devices with their start and end apart: 14, of which 8 were waited for; matrix products, arithmetic and copies ran while one was open for 0% of the time, Pallas kernels for 4%

profile of v2, /device:TPU:1, one launch (start us, length us, event | category | flops | bytes accessed | tf_op | source)
XLA Modules:
  0.0 99.4 jit_solution(106939610344532141)
XLA Ops:
  0.6 0.0 copy-start.4
  0.6 0.0 copy-start.5
  0.7 2.1 %collective-permute-start.1 = (bf16[2,8192]{1,0:T(2,128)(2,1)}, bf16[2,8192]{1,0:T(2,128)(2,1)S(1)}, u32[]{:S(2)}, u32[]{:S(2)}) collective-permute-start(bf16[2,8192]{1,0:T(2,128)(2,1)} %refs_0_.1), channel_id=1, source_target_pairs={{0,64},{32,96},{64,0},{96,32},{128,192},{160,224},{192,128},{224,1... | collective-permute-start | bytes 98312 | tf_op jit(solution)/shard_map/ppermute | solution.py:281
  2.8 2.5 %collective-permute-start.2 = (bf16[2,8192]{1,0:T(2,128)(2,1)}, bf16[2,8192]{1,0:T(2,128)(2,1)S(1)}, u32[]{:S(2)}, u32[]{:S(2)}) collective-permute-start(bf16[2,8192]{1,0:T(2,128)(2,1)} %refs_0_.1), channel_id=1, source_target_pairs={{0,128},{32,160},{64,192},{96,224},{128,0},{160,32},{192,64},{224,... | collective-permute-start | bytes 98312 | tf_op jit(solution)/shard_map/ppermute | solution.py:281
  5.2 0.0 collective-permute-start.3
  5.3 3.4 %collective-permute-start = (bf16[2,8192]{1,0:T(2,128)(2,1)}, bf16[2,8192]{1,0:T(2,128)(2,1)S(1)}, u32[]{:S(2)}, u32[]{:S(2)}) collective-permute-start(bf16[2,8192]{1,0:T(2,128)(2,1)} %refs_0_.1), channel_id=1, source_target_pairs={{0,32},{32,0},{64,96},{96,64},{128,160},{160,128},{192,224},{224,1... | collective-permute-start | bytes 98312 | tf_op jit(solution)/shard_map/ppermute | solution.py:281
  8.7 3.6 %near_first.1 = (bf16[32,256,256]{2,1,0:T(8,128)(2,1)S(1)}, bf16[32,256,48]{2,1,0:T(8,128)(2,1)S(1)}, f32[3,32768]{1,0:T(4,128)S(1)}) custom-call(s32[1,32]{1,0:T(1,128)} %counts.7, s32[2,64]{1,0:T(2,128)} %bitcast.18, f32[3,32768]{1,0:T(4,128)} %station_hbm.1, f32[3,8192]{1,0:T(4,128)} %cell_hbm.1), custom_call_target="tpu_custom_call" | custom-call | flops 402653184 | bytes 6291456 | tf_op jit(solution)/shard_map/near_first/pallas_call | solution.py:295
  12.3 0.0 collective-permute-done.1.refs_2_
  12.3 0.0 collective-permute-done.2.refs_4_
  12.3 0.0 collective-permute-done.3.refs_6_
  12.3 2.2 %collective-permute-start.4 = (bf16[2,8192]{1,0:T(2,128)(2,1)S(1)}, bf16[2,8192]{1,0:T(2,128)(2,1)S(1)}, u32[]{:S(2)}, u32[]{:S(2)}) collective-permute-start(bf16[2,8192]{1,0:T(2,128)(2,1)S(1)} %collective-permute-done.1.refs_2_), channel_id=1, source_target_pairs={{0,32},{32,0},{64,96},{96,64},{128,160},{160,128},{192,224},{224,1... | collective-permute-start | bytes 98312 | tf_op jit(solution)/shard_map/ppermute | solution.py:281
  14.5 0.1 collective-permute-start.5
  14.6 0.4 collective-permute-start.6
  15.0 0.0 copy-done.4
  15.0 0.0 copy-done.5
  15.0 0.0 copy-start.3
  15.1 0.0 copy-start.6
  15.1 0.6 near_second.1.refs_11_.second_blocks
  15.6 0.0 collective-permute-done.refs_1_
  15.7 0.0 collective-permute-done.4.refs_3_
  15.7 0.1 collective-permute-done.5.refs_5_
  15.7 0.2 collective-permute-done.6.refs_7_
  15.9 0.7 copy-done
  16.6 0.6 copy-done.1
  17.3 4.2 %forward.1 = bf16[32,16,1024]{2,1,0:T(8,128)(2,1)S(1)} custom-call(s32[1,32]{1,0:T(1,128)S(1)} %copy-done.5, s32[2,64]{1,0:T(2,128)S(1)} %bitcast.20, s32[2,128]{1,0:T(2,128)S(1)} %bitcast.22, bf16[2,8192]{1,0:T(2,128)(2,1)S(1)} %copy-done.3, bf16[2,8192]{1,0:T(2,128)(2,1)S(1)} %collective-permute-done.refs_1_, ...), custom_call_target="tpu_custom_call" | custom-call | tf_op jit(solution)/shard_map/forward/pallas_call | solution.py:329
  21.5 0.0 copy-start.2
  21.5 19.7 %all_to_all.10.parts = bf16[8,4,16,1024]{3,2,1,0:T(8,128)(2,1)S(1)} all-to-all(bf16[8,4,16,1024]{3,2,1,0:T(8,128)(2,1)S(1)} %bitcast.15), channel_id=1, replica_groups={{0,1,2,3,4,5,6,7},{8,9,10,11,12,13,14,15},{16,17,18,19,20,21,22,23},{24..., dimensions={0} | all-to-all | bytes 2097152 | tf_op jit(solution)/shard_map/all_to_all | solution.py:289
  41.2 0.1 share_sum.1.own
  41.3 3.0 %collective-permute-start.7 = (bf16[4,16,1024]{2,1,0:T(8,128)(2,1)S(1)}, bf16[4,16,1024]{2,1,0:T(8,128)(2,1)S(1)}, u32[]{:S(2)}, u32[]{:S(2)}) collective-permute-start(bf16[4,16,1024]{2,1,0:T(8,128)(2,1)S(1)} %share_sum.1.own), channel_id=1, source_target_pairs={{0,8},{1,9},{2,10},{3,11},{4,12},{5,13},{6,14},{7,15},{8,0},{9,1},... | collective-permute-start | bytes 393224 | tf_op jit(solution)/shard_map/ppermute | solution.py:286
  44.3 5.1 %collective-permute-start.8 = (bf16[4,16,1024]{2,1,0:T(8,128)(2,1)S(1)}, bf16[4,16,1024]{2,1,0:T(8,128)(2,1)S(1)}, u32[]{:S(2)}, u32[]{:S(2)}) collective-permute-start(bf16[4,16,1024]{2,1,0:T(8,128)(2,1)S(1)} %share_sum.1.own), channel_id=1, source_target_pairs={{0,16},{1,17},{2,18},{3,19},{4,20},{5,21},{6,22},{7,23},{8,24},{9,... | collective-permute-start | bytes 393224 | tf_op jit(solution)/shard_map/ppermute | solution.py:286
  49.4 0.2 collective-permute-start.9
  49.6 0.3 collective-permute-done.7.one
  49.9 4.1 %collective-permute-done.8.two = bf16[4,16,1024]{2,1,0:T(8,128)(2,1)S(1)} collective-permute-done((bf16[4,16,1024]{2,1,0:T(8,128)(2,1)S(1)}, bf16[4,16,1024]{2,1,0:T(8,128)(2,1)S(1)}, u32[]{:S(2)}, u32[]{:S(2)}) %collective-permute-start.8) | collective-permute-done | bytes 131104 | tf_op jit(solution)/shard_map/ppermute | solution.py:286
  54.0 7.0 %collective-permute-done.9.three = bf16[4,16,1024]{2,1,0:T(8,128)(2,1)S(1)} collective-permute-done((bf16[4,16,1024]{2,1,0:T(8,128)(2,1)S(1)}, bf16[4,16,1024]{2,1,0:T(8,128)(2,1)S(1)}, u32[]{:S(2)}, u32[]{:S(2)}) %collective-permute-start.9) | collective-permute-done | bytes 131104 | tf_op jit(solution)/shard_map/ppermute | solution.py:286
  61.0 0.0 copy-done.2
  61.0 0.9 weigh.1
  61.9 18.9 %all_to_all.11 = bf16[8,4,16,1024]{3,2,1,0:T(8,128)(2,1)S(1)} all-to-all(bf16[8,4,16,1024]{3,2,1,0:T(8,128)(2,1)S(1)} %get-tuple-element.25), channel_id=1, replica_groups={{0,1,2,3,4,5,6,7},{8,9,10,11,12,13,14,15},{16,17,18,19,20,21,22,23},{24..., dimensions={0} | all-to-all | bytes 2097152 | tf_op jit(solution)/shard_map/all_to_all | solution.py:289
  80.8 4.3 %adjoint.1 = (f32[8,8192]{1,0:T(8,128)S(1)}, bf16[8,8192]{1,0:T(8,128)(2,1)S(1)}) custom-call(s32[1,32]{1,0:T(1,128)S(1)} %copy-done.5, s32[2,64]{1,0:T(2,128)S(1)} %bitcast.21, s32[2,128]{1,0:T(2,128)S(1)} %bitcast.23, bf16[32,16,1024]{2,1,0:T(8,128)(2,1)S(1)} %bitcast.16, bf16[16,256,256]{2,1,0:T(8,128)(2,1)S(1)} %bitcast.12, ...), custom_call_target="tpu_custom_call" | custom-call | tf_op jit(solution)/shard_map/adjoint/pallas_call | solution.py:362
  85.1 3.6 %collective-permute-start.10 = (bf16[8,8192]{1,0:T(8,128)(2,1)S(1)}, bf16[8,8192]{1,0:T(8,128)(2,1)S(1)}, u32[]{:S(2)}, u32[]{:S(2)}) collective-permute-start(bf16[8,8192]{1,0:T(8,128)(2,1)S(1)} %get-tuple-element.27), channel_id=1, source_target_pairs={{0,32},{32,0},{64,96},{96,64},{128,160},{160,128},{192,224},{224,1... | collective-permute-start | bytes 393224 | tf_op jit(solution)/shard_map/ppermute | solution.py:281
  88.7 1.0 collective-permute-done.10.swapped
  89.7 0.1 chip_sum.1
  89.8 0.1 collective-permute-start.11
  89.9 4.9 %collective-permute-start.12 = (bf16[2,8192]{1,0:T(2,128)(2,1)S(1)}, bf16[2,8192]{1,0:T(2,128)(2,1)S(1)}, u32[]{:S(2)}, u32[]{:S(2)}) collective-permute-start(bf16[2,8192]{1,0:T(2,128)(2,1)S(1)} %get-tuple-element.30), channel_id=1, source_target_pairs={{0,128},{32,160},{64,192},{96,224},{128,0},{160,32},{192,64},{224,... | collective-permute-start | bytes 98312 | tf_op jit(solution)/shard_map/ppermute | solution.py:281
  94.8 0.0 collective-permute-start.13
  94.8 0.0 collective-permute-done.11
  94.8 1.6 %collective-permute-done.12 = bf16[2,8192]{1,0:T(2,128)(2,1)S(1)} collective-permute-done((bf16[2,8192]{1,0:T(2,128)(2,1)S(1)}, bf16[2,8192]{1,0:T(2,128)(2,1)S(1)}, u32[]{:S(2)}, u32[]{:S(2)}) %collective-permute-start.12) | collective-permute-done | bytes 32800 | tf_op jit(solution)/shard_map/ppermute | solution.py:281
  96.4 2.3 %collective-permute-done.13 = bf16[2,8192]{1,0:T(2,128)(2,1)S(1)} collective-permute-done((bf16[2,8192]{1,0:T(2,128)(2,1)S(1)}, bf16[2,8192]{1,0:T(2,128)(2,1)S(1)}, u32[]{:S(2)}, u32[]{:S(2)}) %collective-permute-start.13) | collective-permute-done | bytes 32800 | tf_op jit(solution)/shard_map/ppermute | solution.py:281
  98.7 0.7 convert_add_fusion
  (4 shorter events, 0.0 us)
Async XLA Ops:
  0.6 14.4 %copy-start.4 = (s32[1,1,64,2]{2,3,1,0:T(2,128)S(1)}, s32[1,1,64,2]{2,3,1,0:T(2,128)}, u32[]{:S(2)}) copy-start(s32[1,1,64,2]{2,3,1,0:T(2,128)} %param.13) | copy-start | bytes 1540
  0.6 14.4 %copy-start.5 = (s32[1,32]{1,0:T(1,128)S(1)}, s32[1,32]{1,0:T(1,128)}, u32[]{:S(2)}) copy-start(s32[1,32]{1,0:T(1,128)} %counts.7) | copy-start | bytes 388
  0.7 11.6 %collective-permute-start.1 = (bf16[2,8192]{1,0:T(2,128)(2,1)}, bf16[2,8192]{1,0:T(2,128)(2,1)S(1)}, u32[]{:S(2)}, u32[]{:S(2)}) collective-permute-start(bf16[2,8192]{1,0:T(2,128)(2,1)} %refs_0_.1), channel_id=1, source_target_pairs={{0,64},{32,96},{64,0},{96,32},{128,192},{160,224},{192,128},{224,1... | collective-permute-start | bytes 98312 | tf_op jit(solution)/shard_map/ppermute | solution.py:281
  2.8 9.5 %collective-permute-start.2 = (bf16[2,8192]{1,0:T(2,128)(2,1)}, bf16[2,8192]{1,0:T(2,128)(2,1)S(1)}, u32[]{:S(2)}, u32[]{:S(2)}) collective-permute-start(bf16[2,8192]{1,0:T(2,128)(2,1)} %refs_0_.1), channel_id=1, source_target_pairs={{0,128},{32,160},{64,192},{96,224},{128,0},{160,32},{192,64},{224,... | collective-permute-start | bytes 98312 | tf_op jit(solution)/shard_map/ppermute | solution.py:281
  5.2 7.1 %collective-permute-start.3 = (bf16[2,8192]{1,0:T(2,128)(2,1)}, bf16[2,8192]{1,0:T(2,128)(2,1)S(1)}, u32[]{:S(2)}, u32[]{:S(2)}) collective-permute-start(bf16[2,8192]{1,0:T(2,128)(2,1)} %refs_0_.1), channel_id=1, source_target_pairs={{0,192},{32,224},{64,128},{96,160},{128,64},{160,96},{192,0},{224,... | collective-permute-start | bytes 98312 | tf_op jit(solution)/shard_map/ppermute | solution.py:281
  5.3 10.4 %collective-permute-start = (bf16[2,8192]{1,0:T(2,128)(2,1)}, bf16[2,8192]{1,0:T(2,128)(2,1)S(1)}, u32[]{:S(2)}, u32[]{:S(2)}) collective-permute-start(bf16[2,8192]{1,0:T(2,128)(2,1)} %refs_0_.1), channel_id=1, source_target_pairs={{0,32},{32,0},{64,96},{96,64},{128,160},{160,128},{192,224},{224,1... | collective-permute-start | bytes 98312 | tf_op jit(solution)/shard_map/ppermute | solution.py:281
  12.3 3.4 %collective-permute-start.4 = (bf16[2,8192]{1,0:T(2,128)(2,1)S(1)}, bf16[2,8192]{1,0:T(2,128)(2,1)S(1)}, u32[]{:S(2)}, u32[]{:S(2)}) collective-permute-start(bf16[2,8192]{1,0:T(2,128)(2,1)S(1)} %collective-permute-done.1.refs_2_), channel_id=1, source_target_pairs={{0,32},{32,0},{64,96},{96,64},{128,160},{160,128},{192,224},{224,1... | collective-permute-start | bytes 98312 | tf_op jit(solution)/shard_map/ppermute | solution.py:281
  14.5 1.2 %collective-permute-start.5 = (bf16[2,8192]{1,0:T(2,128)(2,1)S(1)}, bf16[2,8192]{1,0:T(2,128)(2,1)S(1)}, u32[]{:S(2)}, u32[]{:S(2)}) collective-permute-start(bf16[2,8192]{1,0:T(2,128)(2,1)S(1)} %collective-permute-done.2.refs_4_), channel_id=1, source_target_pairs={{0,32},{32,0},{64,96},{96,64},{128,160},{160,128},{192,224},{224,1... | collective-permute-start | bytes 98312 | tf_op jit(solution)/shard_map/ppermute | solution.py:281
  14.6 1.3 %collective-permute-start.6 = (bf16[2,8192]{1,0:T(2,128)(2,1)S(1)}, bf16[2,8192]{1,0:T(2,128)(2,1)S(1)}, u32[]{:S(2)}, u32[]{:S(2)}) collective-permute-start(bf16[2,8192]{1,0:T(2,128)(2,1)S(1)} %collective-permute-done.3.refs_6_), channel_id=1, source_target_pairs={{0,32},{32,0},{64,96},{96,64},{128,160},{160,128},{192,224},{224,1... | collective-permute-start | bytes 98312 | tf_op jit(solution)/shard_map/ppermute | solution.py:281
  15.0 1.6 %copy-start = (bf16[1,1,128,32,256]{4,3,2,1,0:T(8,128)(2,1)S(1)}, bf16[1,1,128,32,256]{4,3,2,1,0:T(8,128)(2,1)}, u32[]{:S(2)}) copy-start(bf16[1,1,128,32,256]{4,3,2,1,0:T(8,128)(2,1)} %param.16) | copy-start | bytes 6291460
  15.0 2.2 %copy-start.1 = (bf16[1,1,128,32,256]{4,3,2,1,0:T(8,128)(2,1)S(1)}, bf16[1,1,128,32,256]{4,3,2,1,0:T(8,128)(2,1)}, u32[]{:S(2)}) copy-start(bf16[1,1,128,32,256]{4,3,2,1,0:T(8,128)(2,1)} %param.17) | copy-start | bytes 6291460
  15.0 2.2 %copy-start.3 = (bf16[2,8192]{1,0:T(2,128)(2,1)S(1)}, bf16[2,8192]{1,0:T(2,128)(2,1)}, u32[]{:S(2)}) copy-start(bf16[2,8192]{1,0:T(2,128)(2,1)} %refs_0_.1) | copy-start | bytes 98308
  15.1 2.2 %copy-start.6 = (s32[1,1,128,2]{2,3,1,0:T(2,128)S(1)}, s32[1,1,128,2]{2,3,1,0:T(2,128)}, u32[]{:S(2)}) copy-start(s32[1,1,128,2]{2,3,1,0:T(2,128)} %param.15) | copy-start | bytes 3076
  21.5 39.6 %copy-start.2 = (f32[32768]{0:T(1024)S(1)}, f32[32768]{0:T(1024)}, u32[]{:S(2)}) copy-start(f32[32768]{0:T(1024)} %param.12) | copy-start | bytes 393220
  41.3 8.6 %collective-permute-start.7 = (bf16[4,16,1024]{2,1,0:T(8,128)(2,1)S(1)}, bf16[4,16,1024]{2,1,0:T(8,128)(2,1)S(1)}, u32[]{:S(2)}, u32[]{:S(2)}) collective-permute-start(bf16[4,16,1024]{2,1,0:T(8,128)(2,1)S(1)} %share_sum.1.own), channel_id=1, source_target_pairs={{0,8},{1,9},{2,10},{3,11},{4,12},{5,13},{6,14},{7,15},{8,0},{9,1},... | collective-permute-start | bytes 393224 | tf_op jit(solution)/shard_map/ppermute | solution.py:286
  44.3 9.7 %collective-permute-start.8 = (bf16[4,16,1024]{2,1,0:T(8,128)(2,1)S(1)}, bf16[4,16,1024]{2,1,0:T(8,128)(2,1)S(1)}, u32[]{:S(2)}, u32[]{:S(2)}) collective-permute-start(bf16[4,16,1024]{2,1,0:T(8,128)(2,1)S(1)} %share_sum.1.own), channel_id=1, source_target_pairs={{0,16},{1,17},{2,18},{3,19},{4,20},{5,21},{6,22},{7,23},{8,24},{9,... | collective-permute-start | bytes 393224 | tf_op jit(solution)/shard_map/ppermute | solution.py:286
  49.4 11.7 %collective-permute-start.9 = (bf16[4,16,1024]{2,1,0:T(8,128)(2,1)S(1)}, bf16[4,16,1024]{2,1,0:T(8,128)(2,1)S(1)}, u32[]{:S(2)}, u32[]{:S(2)}) collective-permute-start(bf16[4,16,1024]{2,1,0:T(8,128)(2,1)S(1)} %share_sum.1.own), channel_id=1, source_target_pairs={{0,24},{1,25},{2,26},{3,27},{4,28},{5,29},{6,30},{7,31},{8,16},{9,... | collective-permute-start | bytes 393224 | tf_op jit(solution)/shard_map/ppermute | solution.py:286
  85.1 4.6 %collective-permute-start.10 = (bf16[8,8192]{1,0:T(8,128)(2,1)S(1)}, bf16[8,8192]{1,0:T(8,128)(2,1)S(1)}, u32[]{:S(2)}, u32[]{:S(2)}) collective-permute-start(bf16[8,8192]{1,0:T(8,128)(2,1)S(1)} %get-tuple-element.27), channel_id=1, source_target_pairs={{0,32},{32,0},{64,96},{96,64},{128,160},{160,128},{192,224},{224,1... | collective-permute-start | bytes 393224 | tf_op jit(solution)/shard_map/ppermute | solution.py:281
  89.8 5.0 %collective-permute-start.11 = (bf16[2,8192]{1,0:T(2,128)(2,1)S(1)}, bf16[2,8192]{1,0:T(2,128)(2,1)S(1)}, u32[]{:S(2)}, u32[]{:S(2)}) collective-permute-start(bf16[2,8192]{1,0:T(2,128)(2,1)S(1)} %get-tuple-element.29), channel_id=1, source_target_pairs={{0,64},{32,96},{64,0},{96,32},{128,192},{160,224},{192,128},{224,1... | collective-permute-start | bytes 98312 | tf_op jit(solution)/shard_map/ppermute | solution.py:281
  89.9 6.5 %collective-permute-start.12 = (bf16[2,8192]{1,0:T(2,128)(2,1)S(1)}, bf16[2,8192]{1,0:T(2,128)(2,1)S(1)}, u32[]{:S(2)}, u32[]{:S(2)}) collective-permute-start(bf16[2,8192]{1,0:T(2,128)(2,1)S(1)} %get-tuple-element.30), channel_id=1, source_target_pairs={{0,128},{32,160},{64,192},{96,224},{128,0},{160,32},{192,64},{224,... | collective-permute-start | bytes 98312 | tf_op jit(solution)/shard_map/ppermute | solution.py:281
  94.8 4.0 %collective-permute-start.13 = (bf16[2,8192]{1,0:T(2,128)(2,1)S(1)}, bf16[2,8192]{1,0:T(2,128)(2,1)S(1)}, u32[]{:S(2)}, u32[]{:S(2)}) collective-permute-start(bf16[2,8192]{1,0:T(2,128)(2,1)S(1)} %get-tuple-element.31), channel_id=1, source_target_pairs={{0,192},{32,224},{64,128},{96,160},{128,64},{160,96},{192,0},{224,... | collective-permute-start | bytes 98312 | tf_op jit(solution)/shard_map/ppermute | solution.py:281

commit v3 on v2

--- a/solution.py
+++ b/solution.py
@@ -19,6 +19,7 @@
 WIDE = 8
 TALL = 4
 HALF = 4
+BATCH = 4
 F32 = jnp.float32
 BF16 = jnp.bfloat16
 
@@ -147,18 +148,21 @@
     total[...] = jnp.zeros_like(total)
     mask = block_mask()
 
-    sums = []
-    for g in range(u_ref.shape[0]):
-        source = jnp.concatenate(
-            [vectors[:, lanes_of(mid[1, g * GROUP + j])] for j in range(GROUP)], axis=0
-        )
-        reduced = contract(source, v_ref[g], 1)
-        reduced = jnp.where(mask, reduced, 0.0).astype(BF16)
-        sums.append(contract(reduced, u_ref[g], 0))
-    for g in range(u_ref.shape[0]):
-        for j in range(GROUP):
-            slot, lanes = place(mid[0, g * GROUP + j])
-            total[slot, :, lanes] += sums[g][j * VECS : (j + 1) * VECS]
+    for start in range(0, u_ref.shape[0], BATCH):
+        batch = range(start, start + BATCH)
+        sources = [
+            jnp.concatenate(
+                [vectors[:, lanes_of(mid[1, g * GROUP + j])] for j in range(GROUP)], axis=0
+            )
+            for g in batch
+        ]
+        reduced = [contract(sources[g - start], v_ref[g], 1) for g in batch]
+        reduced = [jnp.where(mask, x, 0.0).astype(BF16) for x in reduced]
+        sums = [contract(reduced[g - start], u_ref[g], 0) for g in batch]
+        for g in batch:
+            for j in range(GROUP):
+                slot, lanes = place(mid[0, g * GROUP + j])
+                total[slot, :, lanes] += sums[g - start][j * VECS : (j + 1) * VECS]
 
     def near_step(g, carry, blocks, first):
         sums = [
@@ -224,18 +228,21 @@
         slot, lanes = place(row)
         return data[slot, :, lanes]
 
-    sums = []
-    for g in range(u_ref.shape[0]):
-        source = jnp.concatenate(
-            [station_tile(mid[0, g * GROUP + j]) for j in range(GROUP)], axis=0
-        )
-        pulled = contract(source, u_ref[g], 1)
-        pulled = jnp.where(mask, pulled, 0.0).astype(BF16)
-        sums.append(contract(pulled, v_ref[g], 0))
-    for g in range(u_ref.shape[0]):
-        for j in range(GROUP):
-            lanes = lanes_of(mid[1, g * GROUP + j])
-            total[:, lanes] += sums[g][j * VECS : (j + 1) * VECS]
+    for start in range(0, u_ref.shape[0], BATCH):
+        batch = range(start, start + BATCH)
+        sources = [
+            jnp.concatenate(
+                [station_tile(mid[0, g * GROUP + j]) for j in range(GROUP)], axis=0
+            )
+            for g in batch
+        ]
+        pulled = [contract(sources[g - start], u_ref[g], 1) for g in batch]
+        pulled = [jnp.where(mask, x, 0.0).astype(BF16) for x in pulled]
+        sums = [contract(pulled[g - start], v_ref[g], 0) for g in batch]
+        for g in batch:
+            for j in range(GROUP):
+                lanes = lanes_of(mid[1, g * GROUP + j])
+                total[:, lanes] += sums[g - start][j * VECS : (j + 1) * VECS]
 
     def near_step(g, carry, blocks, first):
         sums = [

time: 99.3 us -> 95.4 us (0.961)
  Pallas kernels: 13.8 us -> 11.7 us
  starting transfers between devices: 27.6 us -> 26.2 us
  waiting for transfers between devices: 16.7 us -> 15.4 us
    ppermute x3, starting transfers between devices: 8.25 us -> 6.71 us  [over_tall(): return lax.ppermute(x, 'cel', [(i, i ^ WIDE * k) for i in range(32)])]
    pallas_call x1, Pallas kernels: 4.22 us -> 2.79 us  [body(): pl.pallas_call(forward_kernel, in_specs=[SMEM] * 3 + [VMEM] * 12, out_spe...]
    pallas_call x1, Pallas kernels: 4.3 us -> 2.94 us  [body(): pl.pallas_call(adjoint_kernel, in_specs=[SMEM] * 3 + [VMEM] * 5, out_spec...]
  transfers between devices with their start and end apart: 14 -> 14, of which waited for: 8 -> 8; matrix products, arithmetic and copies ran while one was open for 0% -> 0% of each run, Pallas kernels for 4% -> 5%
where the time goes in v3:
time: 95.4 us; the launch traced here: 95.2 us
  blocking collectives  39 us (41%)
  starting transfers between devices  26.2 us (27%)
  waiting for transfers between devices  15.4 us (16%)
  Pallas kernels  11.7 us (12%)
  local copies, waits for them, and re-layouts  1.4 us (1%)
    all_to_all x2, blocking collectives, trade(): return lax.all_to_all(x, axis, 0, 0, axis_index_groups=groups)  39 us
    ppermute x11, starting transfers between devices, over_sta(): return lax.ppermute(x, 'sta', [(i, i ^ k) for i in range(8)])  19.5 us
    ppermute x3, waiting for transfers between devices, over_tall(): return lax.ppermute(x, 'cel', [(i, i ^ WIDE * k) for i in range(32)])  10.8 us
    ppermute x3, starting transfers between devices, over_tall(): return lax.ppermute(x, 'cel', [(i, i ^ WIDE * k) for i in range(32)])  6.71 us
    ppermute x11, waiting for transfers between devices, over_sta(): return lax.ppermute(x, 'sta', [(i, i ^ k) for i in range(8)])  4.64 us
    pallas_call x1, Pallas kernels, body(): pl.pallas_call(near_first_kernel, in_specs=[SMEM] * 2 + [HBM] * 2, out_sp...  4.29 us
    pallas_call x1, Pallas kernels, body(): pl.pallas_call(adjoint_kernel, in_specs=[SMEM] * 3 + [VMEM] * 5, out_spec...  2.94 us
    pallas_call x1, Pallas kernels, body(): pl.pallas_call(forward_kernel, in_specs=[SMEM] * 3 + [VMEM] * 12, out_spe...  2.79 us
  transfers between devices with their start and end apart: 14, of which 8 were waited for; matrix products, arithmetic and copies ran while one was open for 0% of the time, Pallas kernels for 5%

profile of v3, /device:TPU:1, one launch (start us, length us, event | category | flops | bytes accessed | tf_op | source)
XLA Modules:
  0.0 95.2 jit_solution(14094630655822130563)
XLA Ops:
  0.6 0.0 copy-start.4
  0.6 0.0 copy-start.5
  0.7 2.1 %collective-permute-start.1 = (bf16[2,8192]{1,0:T(2,128)(2,1)}, bf16[2,8192]{1,0:T(2,128)(2,1)S(1)}, u32[]{:S(2)}, u32[]{:S(2)}) collective-permute-start(bf16[2,8192]{1,0:T(2,128)(2,1)} %refs_0_.1), channel_id=1, source_target_pairs={{0,64},{32,96},{64,0},{96,32},{128,192},{160,224},{192,128},{224,1... | collective-permute-start | bytes 98312 | tf_op jit(solution)/shard_map/ppermute | solution.py:288
  2.8 2.5 %collective-permute-start.2 = (bf16[2,8192]{1,0:T(2,128)(2,1)}, bf16[2,8192]{1,0:T(2,128)(2,1)S(1)}, u32[]{:S(2)}, u32[]{:S(2)}) collective-permute-start(bf16[2,8192]{1,0:T(2,128)(2,1)} %refs_0_.1), channel_id=1, source_target_pairs={{0,128},{32,160},{64,192},{96,224},{128,0},{160,32},{192,64},{224,... | collective-permute-start | bytes 98312 | tf_op jit(solution)/shard_map/ppermute | solution.py:288
  5.2 0.0 collective-permute-start.3
  5.3 3.4 %collective-permute-start = (bf16[2,8192]{1,0:T(2,128)(2,1)}, bf16[2,8192]{1,0:T(2,128)(2,1)S(1)}, u32[]{:S(2)}, u32[]{:S(2)}) collective-permute-start(bf16[2,8192]{1,0:T(2,128)(2,1)} %refs_0_.1), channel_id=1, source_target_pairs={{0,32},{32,0},{64,96},{96,64},{128,160},{160,128},{192,224},{224,1... | collective-permute-start | bytes 98312 | tf_op jit(solution)/shard_map/ppermute | solution.py:288
  8.7 4.3 %near_first.1 = (bf16[32,256,256]{2,1,0:T(8,128)(2,1)S(1)}, bf16[32,256,48]{2,1,0:T(8,128)(2,1)S(1)}, f32[3,32768]{1,0:T(4,128)S(1)}) custom-call(s32[1,32]{1,0:T(1,128)} %counts.7, s32[2,64]{1,0:T(2,128)} %bitcast.18, f32[3,32768]{1,0:T(4,128)} %station_hbm.1, f32[3,8192]{1,0:T(4,128)} %cell_hbm.1), custom_call_target="tpu_custom_call" | custom-call | flops 402653184 | bytes 6291456 | tf_op jit(solution)/shard_map/near_first/pallas_call | solution.py:302
  13.0 0.0 collective-permute-done.1.refs_2_
  13.0 0.0 collective-permute-done.2.refs_4_
  13.0 0.0 collective-permute-done.3.refs_6_
  13.0 1.5 %collective-permute-start.4 = (bf16[2,8192]{1,0:T(2,128)(2,1)S(1)}, bf16[2,8192]{1,0:T(2,128)(2,1)S(1)}, u32[]{:S(2)}, u32[]{:S(2)}) collective-permute-start(bf16[2,8192]{1,0:T(2,128)(2,1)S(1)} %collective-permute-done.1.refs_2_), channel_id=1, source_target_pairs={{0,32},{32,0},{64,96},{96,64},{128,160},{160,128},{192,224},{224,1... | collective-permute-start | bytes 98312 | tf_op jit(solution)/shard_map/ppermute | solution.py:288
  14.5 0.1 collective-permute-start.5
  14.6 0.4 collective-permute-start.6
  15.0 0.0 copy-done.4
  15.0 0.0 copy-done.5
  15.0 0.0 copy-start.3
  15.1 0.0 copy-start.6
  15.1 0.6 near_second.1.refs_11_.second_blocks
  15.6 0.0 collective-permute-done.refs_1_
  15.7 0.0 collective-permute-done.4.refs_3_
  15.7 0.1 collective-permute-done.5.refs_5_
  15.7 0.2 collective-permute-done.6.refs_7_
  15.9 0.7 copy-done
  16.6 0.6 copy-done.1
  17.3 0.0 copy-done.3
  17.3 2.8 %forward.1 = bf16[32,16,1024]{2,1,0:T(8,128)(2,1)S(1)} custom-call(s32[1,32]{1,0:T(1,128)S(1)} %copy-done.5, s32[2,64]{1,0:T(2,128)S(1)} %bitcast.20, s32[2,128]{1,0:T(2,128)S(1)} %bitcast.22, bf16[2,8192]{1,0:T(2,128)(2,1)S(1)} %copy-done.3, bf16[2,8192]{1,0:T(2,128)(2,1)S(1)} %collective-permute-done.refs_1_, ...), custom_call_target="tpu_custom_call" | custom-call | tf_op jit(solution)/shard_map/forward/pallas_call | solution.py:336
  20.1 0.0 copy-start.2
  20.1 20.8 %all_to_all.10.parts = bf16[8,4,16,1024]{3,2,1,0:T(8,128)(2,1)S(1)} all-to-all(bf16[8,4,16,1024]{3,2,1,0:T(8,128)(2,1)S(1)} %bitcast.15), channel_id=1, replica_groups={{0,1,2,3,4,5,6,7},{8,9,10,11,12,13,14,15},{16,17,18,19,20,21,22,23},{24..., dimensions={0} | all-to-all | bytes 2097152 | tf_op jit(solution)/shard_map/all_to_all | solution.py:296
  40.9 0.1 share_sum.1.own
  41.0 3.3 %collective-permute-start.7 = (bf16[4,16,1024]{2,1,0:T(8,128)(2,1)S(1)}, bf16[4,16,1024]{2,1,0:T(8,128)(2,1)S(1)}, u32[]{:S(2)}, u32[]{:S(2)}) collective-permute-start(bf16[4,16,1024]{2,1,0:T(8,128)(2,1)S(1)} %share_sum.1.own), channel_id=1, source_target_pairs={{0,8},{1,9},{2,10},{3,11},{4,12},{5,13},{6,14},{7,15},{8,0},{9,1},... | collective-permute-start | bytes 393224 | tf_op jit(solution)/shard_map/ppermute | solution.py:293
  44.4 2.9 %collective-permute-start.8 = (bf16[4,16,1024]{2,1,0:T(8,128)(2,1)S(1)}, bf16[4,16,1024]{2,1,0:T(8,128)(2,1)S(1)}, u32[]{:S(2)}, u32[]{:S(2)}) collective-permute-start(bf16[4,16,1024]{2,1,0:T(8,128)(2,1)S(1)} %share_sum.1.own), channel_id=1, source_target_pairs={{0,16},{1,17},{2,18},{3,19},{4,20},{5,21},{6,22},{7,23},{8,24},{9,... | collective-permute-start | bytes 393224 | tf_op jit(solution)/shard_map/ppermute | solution.py:293
  47.3 0.5 collective-permute-start.9
  47.8 2.4 %collective-permute-done.7.one = bf16[4,16,1024]{2,1,0:T(8,128)(2,1)S(1)} collective-permute-done((bf16[4,16,1024]{2,1,0:T(8,128)(2,1)S(1)}, bf16[4,16,1024]{2,1,0:T(8,128)(2,1)S(1)}, u32[]{:S(2)}, u32[]{:S(2)}) %collective-permute-start.7) | collective-permute-done | bytes 131104 | tf_op jit(solution)/shard_map/ppermute | solution.py:293
  50.2 3.3 %collective-permute-done.8.two = bf16[4,16,1024]{2,1,0:T(8,128)(2,1)S(1)} collective-permute-done((bf16[4,16,1024]{2,1,0:T(8,128)(2,1)S(1)}, bf16[4,16,1024]{2,1,0:T(8,128)(2,1)S(1)}, u32[]{:S(2)}, u32[]{:S(2)}) %collective-permute-start.8) | collective-permute-done | bytes 131104 | tf_op jit(solution)/shard_map/ppermute | solution.py:293
  53.5 5.1 %collective-permute-done.9.three = bf16[4,16,1024]{2,1,0:T(8,128)(2,1)S(1)} collective-permute-done((bf16[4,16,1024]{2,1,0:T(8,128)(2,1)S(1)}, bf16[4,16,1024]{2,1,0:T(8,128)(2,1)S(1)}, u32[]{:S(2)}, u32[]{:S(2)}) %collective-permute-start.9) | collective-permute-done | bytes 131104 | tf_op jit(solution)/shard_map/ppermute | solution.py:293
  58.5 0.9 weigh.1
  59.4 18.1 %all_to_all.11 = bf16[8,4,16,1024]{3,2,1,0:T(8,128)(2,1)S(1)} all-to-all(bf16[8,4,16,1024]{3,2,1,0:T(8,128)(2,1)S(1)} %get-tuple-element.25), channel_id=1, replica_groups={{0,1,2,3,4,5,6,7},{8,9,10,11,12,13,14,15},{16,17,18,19,20,21,22,23},{24..., dimensions={0} | all-to-all | bytes 2097152 | tf_op jit(solution)/shard_map/all_to_all | solution.py:296
  77.6 2.9 %adjoint.1 = (f32[8,8192]{1,0:T(8,128)S(1)}, bf16[8,8192]{1,0:T(8,128)(2,1)S(1)}) custom-call(s32[1,32]{1,0:T(1,128)S(1)} %copy-done.5, s32[2,64]{1,0:T(2,128)S(1)} %bitcast.21, s32[2,128]{1,0:T(2,128)S(1)} %bitcast.23, bf16[32,16,1024]{2,1,0:T(8,128)(2,1)S(1)} %bitcast.16, bf16[16,256,256]{2,1,0:T(8,128)(2,1)S(1)} %bitcast.12, ...), custom_call_target="tpu_custom_call" | custom-call | tf_op jit(solution)/shard_map/adjoint/pallas_call | solution.py:369
  80.5 5.6 %collective-permute-start.10 = (bf16[8,8192]{1,0:T(8,128)(2,1)S(1)}, bf16[8,8192]{1,0:T(8,128)(2,1)S(1)}, u32[]{:S(2)}, u32[]{:S(2)}) collective-permute-start(bf16[8,8192]{1,0:T(8,128)(2,1)S(1)} %get-tuple-element.27), channel_id=1, source_target_pairs={{0,32},{32,0},{64,96},{96,64},{128,160},{160,128},{192,224},{224,1... | collective-permute-start | bytes 393224 | tf_op jit(solution)/shard_map/ppermute | solution.py:288
  86.1 1.0 %collective-permute-done.10.swapped = bf16[8,8192]{1,0:T(8,128)(2,1)S(1)} collective-permute-done((bf16[8,8192]{1,0:T(8,128)(2,1)S(1)}, bf16[8,8192]{1,0:T(8,128)(2,1)S(1)}, u32[]{:S(2)}, u32[]{:S(2)}) %collective-permute-start.10) | collective-permute-done | bytes 131104 | tf_op jit(solution)/shard_map/ppermute | solution.py:288
  87.1 0.1 chip_sum.1
  87.1 0.1 collective-permute-start.11
  87.2 3.3 %collective-permute-start.12 = (bf16[2,8192]{1,0:T(2,128)(2,1)S(1)}, bf16[2,8192]{1,0:T(2,128)(2,1)S(1)}, u32[]{:S(2)}, u32[]{:S(2)}) collective-permute-start(bf16[2,8192]{1,0:T(2,128)(2,1)S(1)} %get-tuple-element.30), channel_id=1, source_target_pairs={{0,128},{32,160},{64,192},{96,224},{128,0},{160,32},{192,64},{224,... | collective-permute-start | bytes 98312 | tf_op jit(solution)/shard_map/ppermute | solution.py:288
  90.5 0.6 collective-permute-start.13
  91.1 0.0 collective-permute-done.11
  91.1 1.1 %collective-permute-done.12 = bf16[2,8192]{1,0:T(2,128)(2,1)S(1)} collective-permute-done((bf16[2,8192]{1,0:T(2,128)(2,1)S(1)}, bf16[2,8192]{1,0:T(2,128)(2,1)S(1)}, u32[]{:S(2)}, u32[]{:S(2)}) %collective-permute-start.12) | collective-permute-done | bytes 32800 | tf_op jit(solution)/shard_map/ppermute | solution.py:288
  92.2 2.3 %collective-permute-done.13 = bf16[2,8192]{1,0:T(2,128)(2,1)S(1)} collective-permute-done((bf16[2,8192]{1,0:T(2,128)(2,1)S(1)}, bf16[2,8192]{1,0:T(2,128)(2,1)S(1)}, u32[]{:S(2)}, u32[]{:S(2)}) %collective-permute-start.13) | collective-permute-done | bytes 32800 | tf_op jit(solution)/shard_map/ppermute | solution.py:288
  94.5 0.7 convert_add_fusion
  (4 shorter events, 0.0 us)
Async XLA Ops:
  0.6 14.4 %copy-start.4 = (s32[1,1,64,2]{2,3,1,0:T(2,128)S(1)}, s32[1,1,64,2]{2,3,1,0:T(2,128)}, u32[]{:S(2)}) copy-start(s32[1,1,64,2]{2,3,1,0:T(2,128)} %param.13) | copy-start | bytes 1540
  0.6 14.4 %copy-start.5 = (s32[1,32]{1,0:T(1,128)S(1)}, s32[1,32]{1,0:T(1,128)}, u32[]{:S(2)}) copy-start(s32[1,32]{1,0:T(1,128)} %counts.7) | copy-start | bytes 388
  0.7 12.3 %collective-permute-start.1 = (bf16[2,8192]{1,0:T(2,128)(2,1)}, bf16[2,8192]{1,0:T(2,128)(2,1)S(1)}, u32[]{:S(2)}, u32[]{:S(2)}) collective-permute-start(bf16[2,8192]{1,0:T(2,128)(2,1)} %refs_0_.1), channel_id=1, source_target_pairs={{0,64},{32,96},{64,0},{96,32},{128,192},{160,224},{192,128},{224,1... | collective-permute-start | bytes 98312 | tf_op jit(solution)/shard_map/ppermute | solution.py:288
  2.8 10.2 %collective-permute-start.2 = (bf16[2,8192]{1,0:T(2,128)(2,1)}, bf16[2,8192]{1,0:T(2,128)(2,1)S(1)}, u32[]{:S(2)}, u32[]{:S(2)}) collective-permute-start(bf16[2,8192]{1,0:T(2,128)(2,1)} %refs_0_.1), channel_id=1, source_target_pairs={{0,128},{32,160},{64,192},{96,224},{128,0},{160,32},{192,64},{224,... | collective-permute-start | bytes 98312 | tf_op jit(solution)/shard_map/ppermute | solution.py:288
  5.2 7.8 %collective-permute-start.3 = (bf16[2,8192]{1,0:T(2,128)(2,1)}, bf16[2,8192]{1,0:T(2,128)(2,1)S(1)}, u32[]{:S(2)}, u32[]{:S(2)}) collective-permute-start(bf16[2,8192]{1,0:T(2,128)(2,1)} %refs_0_.1), channel_id=1, source_target_pairs={{0,192},{32,224},{64,128},{96,160},{128,64},{160,96},{192,0},{224,... | collective-permute-start | bytes 98312 | tf_op jit(solution)/shard_map/ppermute | solution.py:288
  5.3 10.4 %collective-permute-start = (bf16[2,8192]{1,0:T(2,128)(2,1)}, bf16[2,8192]{1,0:T(2,128)(2,1)S(1)}, u32[]{:S(2)}, u32[]{:S(2)}) collective-permute-start(bf16[2,8192]{1,0:T(2,128)(2,1)} %refs_0_.1), channel_id=1, source_target_pairs={{0,32},{32,0},{64,96},{96,64},{128,160},{160,128},{192,224},{224,1... | collective-permute-start | bytes 98312 | tf_op jit(solution)/shard_map/ppermute | solution.py:288
  13.0 2.6 %collective-permute-start.4 = (bf16[2,8192]{1,0:T(2,128)(2,1)S(1)}, bf16[2,8192]{1,0:T(2,128)(2,1)S(1)}, u32[]{:S(2)}, u32[]{:S(2)}) collective-permute-start(bf16[2,8192]{1,0:T(2,128)(2,1)S(1)} %collective-permute-done.1.refs_2_), channel_id=1, source_target_pairs={{0,32},{32,0},{64,96},{96,64},{128,160},{160,128},{192,224},{224,1... | collective-permute-start | bytes 98312 | tf_op jit(solution)/shard_map/ppermute | solution.py:288
  14.5 1.2 %collective-permute-start.5 = (bf16[2,8192]{1,0:T(2,128)(2,1)S(1)}, bf16[2,8192]{1,0:T(2,128)(2,1)S(1)}, u32[]{:S(2)}, u32[]{:S(2)}) collective-permute-start(bf16[2,8192]{1,0:T(2,128)(2,1)S(1)} %collective-permute-done.2.refs_4_), channel_id=1, source_target_pairs={{0,32},{32,0},{64,96},{96,64},{128,160},{160,128},{192,224},{224,1... | collective-permute-start | bytes 98312 | tf_op jit(solution)/shard_map/ppermute | solution.py:288
  14.6 1.3 %collective-permute-start.6 = (bf16[2,8192]{1,0:T(2,128)(2,1)S(1)}, bf16[2,8192]{1,0:T(2,128)(2,1)S(1)}, u32[]{:S(2)}, u32[]{:S(2)}) collective-permute-start(bf16[2,8192]{1,0:T(2,128)(2,1)S(1)} %collective-permute-done.3.refs_6_), channel_id=1, source_target_pairs={{0,32},{32,0},{64,96},{96,64},{128,160},{160,128},{192,224},{224,1... | collective-permute-start | bytes 98312 | tf_op jit(solution)/shard_map/ppermute | solution.py:288
  15.0 1.6 %copy-start = (bf16[1,1,128,32,256]{4,3,2,1,0:T(8,128)(2,1)S(1)}, bf16[1,1,128,32,256]{4,3,2,1,0:T(8,128)(2,1)}, u32[]{:S(2)}) copy-start(bf16[1,1,128,32,256]{4,3,2,1,0:T(8,128)(2,1)} %param.16) | copy-start | bytes 6291460
  15.0 2.2 %copy-start.1 = (bf16[1,1,128,32,256]{4,3,2,1,0:T(8,128)(2,1)S(1)}, bf16[1,1,128,32,256]{4,3,2,1,0:T(8,128)(2,1)}, u32[]{:S(2)}) copy-start(bf16[1,1,128,32,256]{4,3,2,1,0:T(8,128)(2,1)} %param.17) | copy-start | bytes 6291460
  15.0 2.2 %copy-start.3 = (bf16[2,8192]{1,0:T(2,128)(2,1)S(1)}, bf16[2,8192]{1,0:T(2,128)(2,1)}, u32[]{:S(2)}) copy-start(bf16[2,8192]{1,0:T(2,128)(2,1)} %refs_0_.1) | copy-start | bytes 98308
  15.1 2.2 %copy-start.6 = (s32[1,1,128,2]{2,3,1,0:T(2,128)S(1)}, s32[1,1,128,2]{2,3,1,0:T(2,128)}, u32[]{:S(2)}) copy-start(s32[1,1,128,2]{2,3,1,0:T(2,128)} %param.15) | copy-start | bytes 3076
  20.1 38.5 %copy-start.2 = (f32[32768]{0:T(1024)S(1)}, f32[32768]{0:T(1024)}, u32[]{:S(2)}) copy-start(f32[32768]{0:T(1024)} %param.12) | copy-start | bytes 393220
  41.0 9.1 %collective-permute-start.7 = (bf16[4,16,1024]{2,1,0:T(8,128)(2,1)S(1)}, bf16[4,16,1024]{2,1,0:T(8,128)(2,1)S(1)}, u32[]{:S(2)}, u32[]{:S(2)}) collective-permute-start(bf16[4,16,1024]{2,1,0:T(8,128)(2,1)S(1)} %share_sum.1.own), channel_id=1, source_target_pairs={{0,8},{1,9},{2,10},{3,11},{4,12},{5,13},{6,14},{7,15},{8,0},{9,1},... | collective-permute-start | bytes 393224 | tf_op jit(solution)/shard_map/ppermute | solution.py:293
  44.4 9.1 %collective-permute-start.8 = (bf16[4,16,1024]{2,1,0:T(8,128)(2,1)S(1)}, bf16[4,16,1024]{2,1,0:T(8,128)(2,1)S(1)}, u32[]{:S(2)}, u32[]{:S(2)}) collective-permute-start(bf16[4,16,1024]{2,1,0:T(8,128)(2,1)S(1)} %share_sum.1.own), channel_id=1, source_target_pairs={{0,16},{1,17},{2,18},{3,19},{4,20},{5,21},{6,22},{7,23},{8,24},{9,... | collective-permute-start | bytes 393224 | tf_op jit(solution)/shard_map/ppermute | solution.py:293
  47.3 11.3 %collective-permute-start.9 = (bf16[4,16,1024]{2,1,0:T(8,128)(2,1)S(1)}, bf16[4,16,1024]{2,1,0:T(8,128)(2,1)S(1)}, u32[]{:S(2)}, u32[]{:S(2)}) collective-permute-start(bf16[4,16,1024]{2,1,0:T(8,128)(2,1)S(1)} %share_sum.1.own), channel_id=1, source_target_pairs={{0,24},{1,25},{2,26},{3,27},{4,28},{5,29},{6,30},{7,31},{8,16},{9,... | collective-permute-start | bytes 393224 | tf_op jit(solution)/shard_map/ppermute | solution.py:293
  80.5 6.5 %collective-permute-start.10 = (bf16[8,8192]{1,0:T(8,128)(2,1)S(1)}, bf16[8,8192]{1,0:T(8,128)(2,1)S(1)}, u32[]{:S(2)}, u32[]{:S(2)}) collective-permute-start(bf16[8,8192]{1,0:T(8,128)(2,1)S(1)} %get-tuple-element.27), channel_id=1, source_target_pairs={{0,32},{32,0},{64,96},{96,64},{128,160},{160,128},{192,224},{224,1... | collective-permute-start | bytes 393224 | tf_op jit(solution)/shard_map/ppermute | solution.py:288
  87.1 3.9 %collective-permute-start.11 = (bf16[2,8192]{1,0:T(2,128)(2,1)S(1)}, bf16[2,8192]{1,0:T(2,128)(2,1)S(1)}, u32[]{:S(2)}, u32[]{:S(2)}) collective-permute-start(bf16[2,8192]{1,0:T(2,128)(2,1)S(1)} %get-tuple-element.29), channel_id=1, source_target_pairs={{0,64},{32,96},{64,0},{96,32},{128,192},{160,224},{192,128},{224,1... | collective-permute-start | bytes 98312 | tf_op jit(solution)/shard_map/ppermute | solution.py:288
  87.2 4.9 %collective-permute-start.12 = (bf16[2,8192]{1,0:T(2,128)(2,1)S(1)}, bf16[2,8192]{1,0:T(2,128)(2,1)S(1)}, u32[]{:S(2)}, u32[]{:S(2)}) collective-permute-start(bf16[2,8192]{1,0:T(2,128)(2,1)S(1)} %get-tuple-element.30), channel_id=1, source_target_pairs={{0,128},{32,160},{64,192},{96,224},{128,0},{160,32},{192,64},{224,... | collective-permute-start | bytes 98312 | tf_op jit(solution)/shard_map/ppermute | solution.py:288
  90.5 4.0 %collective-permute-start.13 = (bf16[2,8192]{1,0:T(2,128)(2,1)S(1)}, bf16[2,8192]{1,0:T(2,128)(2,1)S(1)}, u32[]{:S(2)}, u32[]{:S(2)}) collective-permute-start(bf16[2,8192]{1,0:T(2,128)(2,1)S(1)} %get-tuple-element.31), channel_id=1, source_target_pairs={{0,192},{32,224},{64,128},{96,160},{128,64},{160,96},{192,0},{224,... | collective-permute-start | bytes 98312 | tf_op jit(solution)/shard_map/ppermute | solution.py:288

commit v4 on v3

--- a/solution.py
+++ b/solution.py
@@ -182,40 +182,38 @@
     out[...] = total[...].astype(BF16)
 
 
-def sum_of(parts):
-    total = parts[0].astype(F32)
-    for k in range(1, parts.shape[0]):
-        total = total + parts[k].astype(F32)
-    return total
-
-
-def share_sum_kernel(parts, out):
-    out[...] = sum_of(parts).astype(BF16)
+def share_sum_kernel(parts, *outs):
+    row = lax.axis_index("cel") // WIDE
+    for k in range(TALL):
+        total = parts[0, row ^ k].astype(F32)
+        for w in range(1, WIDE):
+            total = total + parts[w, row ^ k].astype(F32)
+        outs[k][...] = total.astype(outs[k].dtype)
 
 
 def weigh_kernel(own, one, two, three, weights, predicted, weighted):
     sta, cel = lax.axis_index("sta"), lax.axis_index("cel")
-    for h in range(TALL):
-        total = own[h].astype(F32) + one[h].astype(F32)
-        total = total + (two[h].astype(F32) + three[h].astype(F32))
-
-        @pl.when(cel // WIDE == h)
+    total = own[...] + one[...].astype(F32) + two[...].astype(F32) + three[...].astype(F32)
+    scale = weights[pl.ds(pl.multiple_of(cel * 8, 8), 8), :]
+    for r in range(8):
+        at = slice(r * 128, (r + 1) * 128)
+        weighted[:, at] = (total[:, at] * scale[r : r + 1, :]).astype(BF16)
+    for place_of in range(8):
+
+        @pl.when(sta == place_of)
         def _():
-            for place_of in range(8):
-
-                @pl.when(sta == place_of)
-                def _():
-                    for k in range(8):
-                        line = 2 * (k ^ place_of)
-                        predicted[line : line + 2, :] = total[2 * k : 2 * k + 2]
-
-        share = h * WIDE + cel % WIDE
-        scale = weights[pl.ds(pl.multiple_of(share * 8, 8), 8), :]
-        for r in range(8):
-            at = slice(r * 128, (r + 1) * 128)
-            value = (total[:, at] * scale[r : r + 1, :]).astype(BF16)
-            for i in range(WIDE):
-                weighted[i, h, :, at] = value
+            for k in range(8):
+                line = 2 * (k ^ place_of)
+                predicted[line : line + 2, :] = total[2 * k : 2 * k + 2]
+
+
+def copies_kernel(*refs):
+    columns, out = refs[:TALL], refs[TALL]
+    row = lax.axis_index("cel") // WIDE
+    for k in range(TALL):
+        value = columns[k][...]
+        for w in range(WIDE):
+            out[w, row ^ k] = value
 
 
 def adjoint_kernel(
@@ -332,7 +330,6 @@
     )(near_count, near, stations, features)
 
     wide = jax.ShapeDtypeStruct((WIDE, TALL, VECS, 1024), BF16)
-    tall = jax.ShapeDtypeStruct((TALL, VECS, 1024), BF16)
     shares = pl.pallas_call(
         forward_kernel,
         in_specs=[SMEM] * 3 + [VMEM] * 12,
@@ -347,11 +344,13 @@
         name="forward",
     )(near_count, near, mid, *vector_parts, u_factor, v_factor, first_blocks, second_blocks)
 
+    narrow = jax.ShapeDtypeStruct((VECS, 1024), BF16)
+    full = jax.ShapeDtypeStruct((VECS, 1024), F32)
     sums = pl.pallas_call(
         share_sum_kernel,
         in_specs=[VMEM],
-        out_specs=VMEM,
-        out_shape=tall,
+        out_specs=[VMEM] * TALL,
+        out_shape=[full] + [narrow] * (TALL - 1),
         compiler_params=params(8),
         name="share_sum",
     )(trade(shares.reshape(wide.shape), "cel", wide_groups))
@@ -359,11 +358,19 @@
         weigh_kernel,
         in_specs=[VMEM] * 5,
         out_specs=[VMEM] * 2,
-        out_shape=[jax.ShapeDtypeStruct((VECS, 1024), F32), wide],
+        out_shape=[full, narrow],
         compiler_params=params(8),
         name="weigh",
-    )(sums, *[over_tall(sums, k) for k in range(1, TALL)], weights.reshape(-1, 128))
-    data = trade(weighted, "cel", wide_groups).reshape(32, VECS, 1024)
+    )(sums[0], *[over_tall(sums[k], k) for k in range(1, TALL)], weights.reshape(-1, 128))
+    copies = pl.pallas_call(
+        copies_kernel,
+        in_specs=[VMEM] * TALL,
+        out_specs=VMEM,
+        out_shape=wide,
+        compiler_params=params(8),
+        name="copies",
+    )(weighted, *[over_tall(weighted, k) for k in range(1, TALL)])
+    data = trade(copies, "cel", wide_groups).reshape(32, VECS, 1024)
 
     lines = jax.ShapeDtypeStruct((8, 8192), BF16)
     kept, swapped = pl.pallas_call(

time: 95.4 us -> 97.8 us (1.025); the launches traced: 95.2 us -> 96.1 us
  starting transfers between devices: 26.2 us -> 37.2 us
  blocking collectives: 39 us -> 28.5 us
  Pallas kernels: 11.7 us -> 14.3 us
  waiting for transfers between devices: 15.4 us -> 13.5 us
    ppermute x3 -> x6, starting transfers between devices: 6.71 us -> 18.5 us  [over_tall(): return lax.ppermute(x, 'cel', [(i, i ^ WIDE * k) for i in range(32)])]
    all_to_all x2, blocking collectives: 39 us -> 28.5 us  [trade(): return lax.all_to_all(x, axis, 0, 0, axis_index_groups=groups)]
    ppermute x3 -> x6, waiting for transfers between devices: 10.8 us -> 8.1 us  [over_tall(): return lax.ppermute(x, 'cel', [(i, i ^ WIDE * k) for i in range(32)])]
    pallas_call x1, Pallas kernels: 4.29 us -> 5.71 us  [body(): pl.pallas_call(near_first_kernel, in_specs=[SMEM] * 2 + [HBM] * 2, out_sp...]
  transfers between devices with their start and end apart: 14 -> 17, of which waited for: 8 -> 8; matrix products, arithmetic and copies ran while one was open for 0% -> 0% of each run, Pallas kernels for 5% -> 7%
where the time goes in v4:
time: 97.8 us; the launch traced here: 96.1 us
  starting transfers between devices  37.2 us (38%)
  blocking collectives  28.5 us (29%)
  Pallas kernels  14.3 us (15%)
  waiting for transfers between devices  13.5 us (14%)
  local copies, waits for them, and re-layouts  1.15 us (1%)
    all_to_all x2, blocking collectives, trade(): return lax.all_to_all(x, axis, 0, 0, axis_index_groups=groups)  28.5 us
    ppermute x11, starting transfers between devices, over_sta(): return lax.ppermute(x, 'sta', [(i, i ^ k) for i in range(8)])  18.7 us
    ppermute x6, starting transfers between devices, over_tall(): return lax.ppermute(x, 'cel', [(i, i ^ WIDE * k) for i in range(32)])  18.5 us
    ppermute x6, waiting for transfers between devices, over_tall(): return lax.ppermute(x, 'cel', [(i, i ^ WIDE * k) for i in range(32)])  8.1 us
    pallas_call x1, Pallas kernels, body(): pl.pallas_call(near_first_kernel, in_specs=[SMEM] * 2 + [HBM] * 2, out_sp...  5.71 us
    ppermute x11, waiting for transfers between devices, over_sta(): return lax.ppermute(x, 'sta', [(i, i ^ k) for i in range(8)])  5.44 us
    pallas_call x1, Pallas kernels, body(): pl.pallas_call(adjoint_kernel, in_specs=[SMEM] * 3 + [VMEM] * 5, out_spec...  3.72 us
    pallas_call x1, Pallas kernels, body(): pl.pallas_call(forward_kernel, in_specs=[SMEM] * 3 + [VMEM] * 12, out_spe...  3.3 us
  transfers between devices with their start and end apart: 17, of which 8 were waited for; matrix products, arithmetic and copies ran while one was open for 0% of the time, Pallas kernels for 7%

profile of v4, /device:TPU:1, one launch (start us, length us, event | category | flops | bytes accessed | tf_op | source)
XLA Modules:
  0.0 96.1 jit_solution(2530995729838592544)
XLA Ops:
  0.7 2.1 %collective-permute-start.1 = (bf16[2,8192]{1,0:T(2,128)(2,1)}, bf16[2,8192]{1,0:T(2,128)(2,1)S(1)}, u32[]{:S(2)}, u32[]{:S(2)}) collective-permute-start(bf16[2,8192]{1,0:T(2,128)(2,1)} %refs_0_.1), channel_id=1, source_target_pairs={{0,64},{32,96},{64,0},{96,32},{128,192},{160,224},{192,128},{224,1... | collective-permute-start | bytes 98312 | tf_op jit(solution)/shard_map/ppermute | solution.py:286
  2.8 2.5 %collective-permute-start.2 = (bf16[2,8192]{1,0:T(2,128)(2,1)}, bf16[2,8192]{1,0:T(2,128)(2,1)S(1)}, u32[]{:S(2)}, u32[]{:S(2)}) collective-permute-start(bf16[2,8192]{1,0:T(2,128)(2,1)} %refs_0_.1), channel_id=1, source_target_pairs={{0,128},{32,160},{64,192},{96,224},{128,0},{160,32},{192,64},{224,... | collective-permute-start | bytes 98312 | tf_op jit(solution)/shard_map/ppermute | solution.py:286
  5.2 0.0 collective-permute-start.3
  5.3 3.4 %collective-permute-start = (bf16[2,8192]{1,0:T(2,128)(2,1)}, bf16[2,8192]{1,0:T(2,128)(2,1)S(1)}, u32[]{:S(2)}, u32[]{:S(2)}) collective-permute-start(bf16[2,8192]{1,0:T(2,128)(2,1)} %refs_0_.1), channel_id=1, source_target_pairs={{0,32},{32,0},{64,96},{96,64},{128,160},{160,128},{192,224},{224,1... | collective-permute-start | bytes 98312 | tf_op jit(solution)/shard_map/ppermute | solution.py:286
  8.7 5.7 %near_first.1 = (bf16[32,256,256]{2,1,0:T(8,128)(2,1)S(1)}, bf16[32,256,48]{2,1,0:T(8,128)(2,1)S(1)}, f32[3,32768]{1,0:T(4,128)S(1)}) custom-call(s32[1,32]{1,0:T(1,128)} %counts.7, s32[2,64]{1,0:T(2,128)} %bitcast.18, f32[3,32768]{1,0:T(4,128)} %station_hbm.1, f32[3,8192]{1,0:T(4,128)} %cell_hbm.1), custom_call_target="tpu_custom_call" | custom-call | flops 402653184 | bytes 6291456 | tf_op jit(solution)/shard_map/near_first/pallas_call | solution.py:300
  14.4 0.0 collective-permute-done.1.refs_2_
  14.4 0.0 collective-permute-done.2.refs_4_
  14.4 0.0 collective-permute-done.3.refs_6_
  14.4 0.1 collective-permute-start.4
  14.5 0.5 collective-permute-start.5
  15.0 0.1 collective-permute-start.6
  15.1 0.0 copy-start.3
  15.2 0.0 copy-start.6
  15.2 0.6 near_second.1.refs_11_.second_blocks
  15.8 0.0 collective-permute-done.refs_1_
  15.8 0.0 collective-permute-done.4.refs_3_
  15.8 0.1 collective-permute-done.5.refs_5_
  15.9 0.3 collective-permute-done.6.refs_7_
  16.2 0.5 copy-done
  16.7 0.6 copy-done.1
  17.4 3.3 %forward.1 = bf16[32,16,1024]{2,1,0:T(8,128)(2,1)S(1)} custom-call(s32[1,32]{1,0:T(1,128)S(1)} %copy-done.5, s32[2,64]{1,0:T(2,128)S(1)} %bitcast.20, s32[2,128]{1,0:T(2,128)S(1)} %bitcast.22, bf16[2,8192]{1,0:T(2,128)(2,1)S(1)} %copy-done.3, bf16[2,8192]{1,0:T(2,128)(2,1)S(1)} %collective-permute-done.refs_1_, ...), custom_call_target="tpu_custom_call" | custom-call | tf_op jit(solution)/shard_map/forward/pallas_call | solution.py:333
  20.7 0.0 copy-start.2
  20.7 14.7 %all_to_all.10.parts = bf16[8,4,16,1024]{3,2,1,0:T(8,128)(2,1)S(1)} all-to-all(bf16[8,4,16,1024]{3,2,1,0:T(8,128)(2,1)S(1)} %bitcast.15), channel_id=1, replica_groups={{0,1,2,3,4,5,6,7},{8,9,10,11,12,13,14,15},{16,17,18,19,20,21,22,23},{24..., dimensions={0} | all-to-all | bytes 2097152 | tf_op jit(solution)/shard_map/all_to_all | solution.py:294
  35.4 0.1 share_sum.1
  35.5 8.7 %collective-permute-start.7 = (bf16[16,1024]{1,0:T(8,128)(2,1)S(1)}, bf16[16,1024]{1,0:T(8,128)(2,1)S(1)}, u32[]{:S(2)}, u32[]{:S(2)}) collective-permute-start(bf16[16,1024]{1,0:T(8,128)(2,1)S(1)} %get-tuple-element.29), channel_id=1, source_target_pairs={{0,8},{1,9},{2,10},{3,11},{4,12},{5,13},{6,14},{7,15},{8,0},{9,1},... | collective-permute-start | bytes 98312 | tf_op jit(solution)/shard_map/ppermute | solution.py:291
  44.2 4.2 %collective-permute-start.8 = (bf16[16,1024]{1,0:T(8,128)(2,1)S(1)}, bf16[16,1024]{1,0:T(8,128)(2,1)S(1)}, u32[]{:S(2)}, u32[]{:S(2)}) collective-permute-start(bf16[16,1024]{1,0:T(8,128)(2,1)S(1)} %get-tuple-element.30), channel_id=1, source_target_pairs={{0,16},{1,17},{2,18},{3,19},{4,20},{5,21},{6,22},{7,23},{8,24},{9,... | collective-permute-start | bytes 98312 | tf_op jit(solution)/shard_map/ppermute | solution.py:291
  48.3 0.0 collective-permute-start.9
  48.3 2.5 %collective-permute-done.8.two = bf16[16,1024]{1,0:T(8,128)(2,1)S(1)} collective-permute-done((bf16[16,1024]{1,0:T(8,128)(2,1)S(1)}, bf16[16,1024]{1,0:T(8,128)(2,1)S(1)}, u32[]{:S(2)}, u32[]{:S(2)}) %collective-permute-start.8) | collective-permute-done | bytes 32800 | tf_op jit(solution)/shard_map/ppermute | solution.py:291
  50.9 2.6 %collective-permute-done.9.three = bf16[16,1024]{1,0:T(8,128)(2,1)S(1)} collective-permute-done((bf16[16,1024]{1,0:T(8,128)(2,1)S(1)}, bf16[16,1024]{1,0:T(8,128)(2,1)S(1)}, u32[]{:S(2)}, u32[]{:S(2)}) %collective-permute-start.9) | collective-permute-done | bytes 32800 | tf_op jit(solution)/shard_map/ppermute | solution.py:291
  53.5 0.7 weigh.1
  54.2 1.2 %collective-permute-start.10 = (bf16[16,1024]{1,0:T(8,128)(2,1)S(1)}, bf16[16,1024]{1,0:T(8,128)(2,1)S(1)}, u32[]{:S(2)}, u32[]{:S(2)}) collective-permute-start(bf16[16,1024]{1,0:T(8,128)(2,1)S(1)} %get-tuple-element.33.refs_0_), channel_id=1, source_target_pairs={{0,8},{1,9},{2,10},{3,11},{4,12},{5,13},{6,14},{7,15},{8,0},{9,1},... | collective-permute-start | bytes 98312 | tf_op jit(solution)/shard_map/ppermute | solution.py:291
  55.4 1.0 %collective-permute-start.11 = (bf16[16,1024]{1,0:T(8,128)(2,1)S(1)}, bf16[16,1024]{1,0:T(8,128)(2,1)S(1)}, u32[]{:S(2)}, u32[]{:S(2)}) collective-permute-start(bf16[16,1024]{1,0:T(8,128)(2,1)S(1)} %get-tuple-element.33.refs_0_), channel_id=1, source_target_pairs={{0,16},{1,17},{2,18},{3,19},{4,20},{5,21},{6,22},{7,23},{8,24},{9,... | collective-permute-start | bytes 98312 | tf_op jit(solution)/shard_map/ppermute | solution.py:291
  56.4 3.4 %collective-permute-start.12 = (bf16[16,1024]{1,0:T(8,128)(2,1)S(1)}, bf16[16,1024]{1,0:T(8,128)(2,1)S(1)}, u32[]{:S(2)}, u32[]{:S(2)}) collective-permute-start(bf16[16,1024]{1,0:T(8,128)(2,1)S(1)} %get-tuple-element.33.refs_0_), channel_id=1, source_target_pairs={{0,24},{1,25},{2,26},{3,27},{4,28},{5,29},{6,30},{7,31},{8,16},{9,... | collective-permute-start | bytes 98312 | tf_op jit(solution)/shard_map/ppermute | solution.py:291
  59.9 0.0 collective-permute-done.10.refs_1_
  59.9 2.9 %collective-permute-done.11.refs_2_ = bf16[16,1024]{1,0:T(8,128)(2,1)S(1)} collective-permute-done((bf16[16,1024]{1,0:T(8,128)(2,1)S(1)}, bf16[16,1024]{1,0:T(8,128)(2,1)S(1)}, u32[]{:S(2)}, u32[]{:S(2)}) %collective-permute-start.11) | collective-permute-done | bytes 32800 | tf_op jit(solution)/shard_map/ppermute | solution.py:291
  62.8 0.0 collective-permute-done.12.refs_3_
  62.8 0.1 copies.1
  62.9 13.8 %all_to_all.11 = bf16[8,4,16,1024]{3,2,1,0:T(8,128)(2,1)S(1)} all-to-all(bf16[8,4,16,1024]{3,2,1,0:T(8,128)(2,1)S(1)} %copies.1), channel_id=1, replica_groups={{0,1,2,3,4,5,6,7},{8,9,10,11,12,13,14,15},{16,17,18,19,20,21,22,23},{24..., dimensions={0} | all-to-all | bytes 2097152 | tf_op jit(solution)/shard_map/all_to_all | solution.py:294
  76.7 3.7 %adjoint.1 = (f32[8,8192]{1,0:T(8,128)S(1)}, bf16[8,8192]{1,0:T(8,128)(2,1)S(1)}) custom-call(s32[1,32]{1,0:T(1,128)S(1)} %copy-done.5, s32[2,64]{1,0:T(2,128)S(1)} %bitcast.21, s32[2,128]{1,0:T(2,128)S(1)} %bitcast.23, bf16[32,16,1024]{2,1,0:T(8,128)(2,1)S(1)} %bitcast.16, bf16[16,256,256]{2,1,0:T(8,128)(2,1)S(1)} %bitcast.12, ...), custom_call_target="tpu_custom_call" | custom-call | tf_op jit(solution)/shard_map/adjoint/pallas_call | solution.py:376
  80.4 5.0 %collective-permute-start.13 = (bf16[8,8192]{1,0:T(8,128)(2,1)S(1)}, bf16[8,8192]{1,0:T(8,128)(2,1)S(1)}, u32[]{:S(2)}, u32[]{:S(2)}) collective-permute-start(bf16[8,8192]{1,0:T(8,128)(2,1)S(1)} %get-tuple-element.35), channel_id=1, source_target_pairs={{0,32},{32,0},{64,96},{96,64},{128,160},{160,128},{192,224},{224,1... | collective-permute-start | bytes 393224 | tf_op jit(solution)/shard_map/ppermute | solution.py:286
  85.4 1.0 %collective-permute-done.13.swapped = bf16[8,8192]{1,0:T(8,128)(2,1)S(1)} collective-permute-done((bf16[8,8192]{1,0:T(8,128)(2,1)S(1)}, bf16[8,8192]{1,0:T(8,128)(2,1)S(1)}, u32[]{:S(2)}, u32[]{:S(2)}) %collective-permute-start.13) | collective-permute-done | bytes 131104 | tf_op jit(solution)/shard_map/ppermute | solution.py:286
  86.4 0.1 chip_sum.1
  86.5 0.5 collective-permute-start.14
  87.0 4.5 %collective-permute-start.15 = (bf16[2,8192]{1,0:T(2,128)(2,1)S(1)}, bf16[2,8192]{1,0:T(2,128)(2,1)S(1)}, u32[]{:S(2)}, u32[]{:S(2)}) collective-permute-start(bf16[2,8192]{1,0:T(2,128)(2,1)S(1)} %get-tuple-element.38), channel_id=1, source_target_pairs={{0,128},{32,160},{64,192},{96,224},{128,0},{160,32},{192,64},{224,... | collective-permute-start | bytes 98312 | tf_op jit(solution)/shard_map/ppermute | solution.py:286
  91.4 0.0 collective-permute-start.16
  91.5 1.6 %collective-permute-done.15 = bf16[2,8192]{1,0:T(2,128)(2,1)S(1)} collective-permute-done((bf16[2,8192]{1,0:T(2,128)(2,1)S(1)}, bf16[2,8192]{1,0:T(2,128)(2,1)S(1)}, u32[]{:S(2)}, u32[]{:S(2)}) %collective-permute-start.15) | collective-permute-done | bytes 32800 | tf_op jit(solution)/shard_map/ppermute | solution.py:286
  93.1 2.3 %collective-permute-done.16 = bf16[2,8192]{1,0:T(2,128)(2,1)S(1)} collective-permute-done((bf16[2,8192]{1,0:T(2,128)(2,1)S(1)}, bf16[2,8192]{1,0:T(2,128)(2,1)S(1)}, u32[]{:S(2)}, u32[]{:S(2)}) %collective-permute-start.16) | collective-permute-done | bytes 32800 | tf_op jit(solution)/shard_map/ppermute | solution.py:286
  95.4 0.7 convert_add_fusion
  (11 shorter events, 0.0 us)
Async XLA Ops:
  0.6 14.5 %copy-start.4 = (s32[1,1,64,2]{2,3,1,0:T(2,128)S(1)}, s32[1,1,64,2]{2,3,1,0:T(2,128)}, u32[]{:S(2)}) copy-start(s32[1,1,64,2]{2,3,1,0:T(2,128)} %param.13) | copy-start | bytes 1540
  0.6 14.5 %copy-start.5 = (s32[1,32]{1,0:T(1,128)S(1)}, s32[1,32]{1,0:T(1,128)}, u32[]{:S(2)}) copy-start(s32[1,32]{1,0:T(1,128)} %counts.7) | copy-start | bytes 388
  0.7 13.8 %collective-permute-start.1 = (bf16[2,8192]{1,0:T(2,128)(2,1)}, bf16[2,8192]{1,0:T(2,128)(2,1)S(1)}, u32[]{:S(2)}, u32[]{:S(2)}) collective-permute-start(bf16[2,8192]{1,0:T(2,128)(2,1)} %refs_0_.1), channel_id=1, source_target_pairs={{0,64},{32,96},{64,0},{96,32},{128,192},{160,224},{192,128},{224,1... | collective-permute-start | bytes 98312 | tf_op jit(solution)/shard_map/ppermute | solution.py:286
  2.8 11.6 %collective-permute-start.2 = (bf16[2,8192]{1,0:T(2,128)(2,1)}, bf16[2,8192]{1,0:T(2,128)(2,1)S(1)}, u32[]{:S(2)}, u32[]{:S(2)}) collective-permute-start(bf16[2,8192]{1,0:T(2,128)(2,1)} %refs_0_.1), channel_id=1, source_target_pairs={{0,128},{32,160},{64,192},{96,224},{128,0},{160,32},{192,64},{224,... | collective-permute-start | bytes 98312 | tf_op jit(solution)/shard_map/ppermute | solution.py:286
  5.2 9.2 %collective-permute-start.3 = (bf16[2,8192]{1,0:T(2,128)(2,1)}, bf16[2,8192]{1,0:T(2,128)(2,1)S(1)}, u32[]{:S(2)}, u32[]{:S(2)}) collective-permute-start(bf16[2,8192]{1,0:T(2,128)(2,1)} %refs_0_.1), channel_id=1, source_target_pairs={{0,192},{32,224},{64,128},{96,160},{128,64},{160,96},{192,0},{224,... | collective-permute-start | bytes 98312 | tf_op jit(solution)/shard_map/ppermute | solution.py:286
  5.3 10.5 %collective-permute-start = (bf16[2,8192]{1,0:T(2,128)(2,1)}, bf16[2,8192]{1,0:T(2,128)(2,1)S(1)}, u32[]{:S(2)}, u32[]{:S(2)}) collective-permute-start(bf16[2,8192]{1,0:T(2,128)(2,1)} %refs_0_.1), channel_id=1, source_target_pairs={{0,32},{32,0},{64,96},{96,64},{128,160},{160,128},{192,224},{224,1... | collective-permute-start | bytes 98312 | tf_op jit(solution)/shard_map/ppermute | solution.py:286
  14.4 1.3 %collective-permute-start.4 = (bf16[2,8192]{1,0:T(2,128)(2,1)S(1)}, bf16[2,8192]{1,0:T(2,128)(2,1)S(1)}, u32[]{:S(2)}, u32[]{:S(2)}) collective-permute-start(bf16[2,8192]{1,0:T(2,128)(2,1)S(1)} %collective-permute-done.1.refs_2_), channel_id=1, source_target_pairs={{0,32},{32,0},{64,96},{96,64},{128,160},{160,128},{192,224},{224,1... | collective-permute-start | bytes 98312 | tf_op jit(solution)/shard_map/ppermute | solution.py:286
  14.5 1.4 %collective-permute-start.5 = (bf16[2,8192]{1,0:T(2,128)(2,1)S(1)}, bf16[2,8192]{1,0:T(2,128)(2,1)S(1)}, u32[]{:S(2)}, u32[]{:S(2)}) collective-permute-start(bf16[2,8192]{1,0:T(2,128)(2,1)S(1)} %collective-permute-done.2.refs_4_), channel_id=1, source_target_pairs={{0,32},{32,0},{64,96},{96,64},{128,160},{160,128},{192,224},{224,1... | collective-permute-start | bytes 98312 | tf_op jit(solution)/shard_map/ppermute | solution.py:286
  15.0 1.2 %collective-permute-start.6 = (bf16[2,8192]{1,0:T(2,128)(2,1)S(1)}, bf16[2,8192]{1,0:T(2,128)(2,1)S(1)}, u32[]{:S(2)}, u32[]{:S(2)}) collective-permute-start(bf16[2,8192]{1,0:T(2,128)(2,1)S(1)} %collective-permute-done.3.refs_6_), channel_id=1, source_target_pairs={{0,32},{32,0},{64,96},{96,64},{128,160},{160,128},{192,224},{224,1... | collective-permute-start | bytes 98312 | tf_op jit(solution)/shard_map/ppermute | solution.py:286
  15.1 1.6 %copy-start = (bf16[1,1,128,32,256]{4,3,2,1,0:T(8,128)(2,1)S(1)}, bf16[1,1,128,32,256]{4,3,2,1,0:T(8,128)(2,1)}, u32[]{:S(2)}) copy-start(bf16[1,1,128,32,256]{4,3,2,1,0:T(8,128)(2,1)} %param.16) | copy-start | bytes 6291460
  15.1 2.2 %copy-start.1 = (bf16[1,1,128,32,256]{4,3,2,1,0:T(8,128)(2,1)S(1)}, bf16[1,1,128,32,256]{4,3,2,1,0:T(8,128)(2,1)}, u32[]{:S(2)}) copy-start(bf16[1,1,128,32,256]{4,3,2,1,0:T(8,128)(2,1)} %param.17) | copy-start | bytes 6291460
  15.1 2.2 %copy-start.3 = (bf16[2,8192]{1,0:T(2,128)(2,1)S(1)}, bf16[2,8192]{1,0:T(2,128)(2,1)}, u32[]{:S(2)}) copy-start(bf16[2,8192]{1,0:T(2,128)(2,1)} %refs_0_.1) | copy-start | bytes 98308
  15.2 2.2 %copy-start.6 = (s32[1,1,128,2]{2,3,1,0:T(2,128)S(1)}, s32[1,1,128,2]{2,3,1,0:T(2,128)}, u32[]{:S(2)}) copy-start(s32[1,1,128,2]{2,3,1,0:T(2,128)} %param.15) | copy-start | bytes 3076
  20.7 32.8 %copy-start.2 = (f32[32768]{0:T(1024)S(1)}, f32[32768]{0:T(1024)}, u32[]{:S(2)}) copy-start(f32[32768]{0:T(1024)} %param.12) | copy-start | bytes 393220
  35.5 12.8 %collective-permute-start.7 = (bf16[16,1024]{1,0:T(8,128)(2,1)S(1)}, bf16[16,1024]{1,0:T(8,128)(2,1)S(1)}, u32[]{:S(2)}, u32[]{:S(2)}) collective-permute-start(bf16[16,1024]{1,0:T(8,128)(2,1)S(1)} %get-tuple-element.29), channel_id=1, source_target_pairs={{0,8},{1,9},{2,10},{3,11},{4,12},{5,13},{6,14},{7,15},{8,0},{9,1},... | collective-permute-start | bytes 98312 | tf_op jit(solution)/shard_map/ppermute | solution.py:291
  44.2 6.7 %collective-permute-start.8 = (bf16[16,1024]{1,0:T(8,128)(2,1)S(1)}, bf16[16,1024]{1,0:T(8,128)(2,1)S(1)}, u32[]{:S(2)}, u32[]{:S(2)}) collective-permute-start(bf16[16,1024]{1,0:T(8,128)(2,1)S(1)} %get-tuple-element.30), channel_id=1, source_target_pairs={{0,16},{1,17},{2,18},{3,19},{4,20},{5,21},{6,22},{7,23},{8,24},{9,... | collective-permute-start | bytes 98312 | tf_op jit(solution)/shard_map/ppermute | solution.py:291
  48.3 5.2 %collective-permute-start.9 = (bf16[16,1024]{1,0:T(8,128)(2,1)S(1)}, bf16[16,1024]{1,0:T(8,128)(2,1)S(1)}, u32[]{:S(2)}, u32[]{:S(2)}) collective-permute-start(bf16[16,1024]{1,0:T(8,128)(2,1)S(1)} %get-tuple-element.31), channel_id=1, source_target_pairs={{0,24},{1,25},{2,26},{3,27},{4,28},{5,29},{6,30},{7,31},{8,16},{9,... | collective-permute-start | bytes 98312 | tf_op jit(solution)/shard_map/ppermute | solution.py:291
  54.2 5.7 %collective-permute-start.10 = (bf16[16,1024]{1,0:T(8,128)(2,1)S(1)}, bf16[16,1024]{1,0:T(8,128)(2,1)S(1)}, u32[]{:S(2)}, u32[]{:S(2)}) collective-permute-start(bf16[16,1024]{1,0:T(8,128)(2,1)S(1)} %get-tuple-element.33.refs_0_), channel_id=1, source_target_pairs={{0,8},{1,9},{2,10},{3,11},{4,12},{5,13},{6,14},{7,15},{8,0},{9,1},... | collective-permute-start | bytes 98312 | tf_op jit(solution)/shard_map/ppermute | solution.py:291
  55.4 7.4 %collective-permute-start.11 = (bf16[16,1024]{1,0:T(8,128)(2,1)S(1)}, bf16[16,1024]{1,0:T(8,128)(2,1)S(1)}, u32[]{:S(2)}, u32[]{:S(2)}) collective-permute-start(bf16[16,1024]{1,0:T(8,128)(2,1)S(1)} %get-tuple-element.33.refs_0_), channel_id=1, source_target_pairs={{0,16},{1,17},{2,18},{3,19},{4,20},{5,21},{6,22},{7,23},{8,24},{9,... | collective-permute-start | bytes 98312 | tf_op jit(solution)/shard_map/ppermute | solution.py:291
  56.4 6.4 %collective-permute-start.12 = (bf16[16,1024]{1,0:T(8,128)(2,1)S(1)}, bf16[16,1024]{1,0:T(8,128)(2,1)S(1)}, u32[]{:S(2)}, u32[]{:S(2)}) collective-permute-start(bf16[16,1024]{1,0:T(8,128)(2,1)S(1)} %get-tuple-element.33.refs_0_), channel_id=1, source_target_pairs={{0,24},{1,25},{2,26},{3,27},{4,28},{5,29},{6,30},{7,31},{8,16},{9,... | collective-permute-start | bytes 98312 | tf_op jit(solution)/shard_map/ppermute | solution.py:291
  80.4 6.0 %collective-permute-start.13 = (bf16[8,8192]{1,0:T(8,128)(2,1)S(1)}, bf16[8,8192]{1,0:T(8,128)(2,1)S(1)}, u32[]{:S(2)}, u32[]{:S(2)}) collective-permute-start(bf16[8,8192]{1,0:T(8,128)(2,1)S(1)} %get-tuple-element.35), channel_id=1, source_target_pairs={{0,32},{32,0},{64,96},{96,64},{128,160},{160,128},{192,224},{224,1... | collective-permute-start | bytes 393224 | tf_op jit(solution)/shard_map/ppermute | solution.py:286
  86.5 5.0 %collective-permute-start.14 = (bf16[2,8192]{1,0:T(2,128)(2,1)S(1)}, bf16[2,8192]{1,0:T(2,128)(2,1)S(1)}, u32[]{:S(2)}, u32[]{:S(2)}) collective-permute-start(bf16[2,8192]{1,0:T(2,128)(2,1)S(1)} %get-tuple-element.37), channel_id=1, source_target_pairs={{0,64},{32,96},{64,0},{96,32},{128,192},{160,224},{192,128},{224,1... | collective-permute-start | bytes 98312 | tf_op jit(solution)/shard_map/ppermute | solution.py:286
  87.0 6.1 %collective-permute-start.15 = (bf16[2,8192]{1,0:T(2,128)(2,1)S(1)}, bf16[2,8192]{1,0:T(2,128)(2,1)S(1)}, u32[]{:S(2)}, u32[]{:S(2)}) collective-permute-start(bf16[2,8192]{1,0:T(2,128)(2,1)S(1)} %get-tuple-element.38), channel_id=1, source_target_pairs={{0,128},{32,160},{64,192},{96,224},{128,0},{160,32},{192,64},{224,... | collective-permute-start | bytes 98312 | tf_op jit(solution)/shard_map/ppermute | solution.py:286
  91.4 4.0 %collective-permute-start.16 = (bf16[2,8192]{1,0:T(2,128)(2,1)S(1)}, bf16[2,8192]{1,0:T(2,128)(2,1)S(1)}, u32[]{:S(2)}, u32[]{:S(2)}) collective-permute-start(bf16[2,8192]{1,0:T(2,128)(2,1)S(1)} %get-tuple-element.39), channel_id=1, source_target_pairs={{0,192},{32,224},{64,128},{96,160},{128,64},{160,96},{192,0},{224,... | collective-permute-start | bytes 98312 | tf_op jit(solution)/shard_map/ppermute | solution.py:286

commit v5 on v3

--- a/solution.py
+++ b/solution.py
@@ -79,8 +79,8 @@
 
     def cell_chunk(i, carry):
         lines = lax.broadcasted_iota(jnp.int32, (8, TILE), 0)
-        for q in range(4):
-            at = lanes_of(i * 4 + q)
+        for q in range(8):
+            at = lanes_of(i * 8 + q)
             x, y, z = (SHRINK * cells[d : d + 1, at] for d in range(3))
             square = x * x + y * y + z * z
             block = stack(
@@ -95,10 +95,10 @@
                 ),
             )
             h, m, l = split3(block)
-            features[i * 4 + q] = jnp.concatenate((h, h, h, m, m, l), axis=0).T.astype(BF16)
+            features[i * 8 + q] = jnp.concatenate((h, h, h, m, m, l), axis=0).T.astype(BF16)
         return carry
 
-    lax.fori_loop(0, features.shape[0] // 4, cell_chunk, 0)
+    lax.fori_loop(0, features.shape[0] // 8, cell_chunk, 0)
     fetches[1].wait()
 
     def step(g, carry):

time: 95.4 us -> 94.5 us (level); the launches traced: 95.2 us -> 93 us
  Pallas kernels: 11.7 us -> 10 us
    ppermute x11, starting transfers between devices: 19.5 us -> 17.4 us  [over_sta(): return lax.ppermute(x, 'sta', [(i, i ^ k) for i in range(8)])]
    ppermute x3, starting transfers between devices: 6.71 us -> 8.69 us  [over_tall(): return lax.ppermute(x, 'cel', [(i, i ^ WIDE * k) for i in range(32)])]
    pallas_call x1, Pallas kernels: 4.29 us -> 3.25 us  [body(): pl.pallas_call(near_first_kernel, in_specs=[SMEM] * 2 + [HBM] * 2, out_sp...]
  transfers between devices with their start and end apart: 14 -> 14, of which waited for: 8 -> 8; matrix products, arithmetic and copies ran while one was open for 0% -> 0% of each run, Pallas kernels for 5% -> 4%
where the time goes in v5:
time: 94.5 us; the launch traced here: 93 us
  blocking collectives  38.4 us (41%)
  starting transfers between devices  26.1 us (28%)
  waiting for transfers between devices  15.9 us (17%)
  Pallas kernels  10 us (11%)
  local copies, waits for them, and re-layouts  1.15 us (1%)
    all_to_all x2, blocking collectives, trade(): return lax.all_to_all(x, axis, 0, 0, axis_index_groups=groups)  38.4 us
    ppermute x11, starting transfers between devices, over_sta(): return lax.ppermute(x, 'sta', [(i, i ^ k) for i in range(8)])  17.4 us
    ppermute x3, waiting for transfers between devices, over_tall(): return lax.ppermute(x, 'cel', [(i, i ^ WIDE * k) for i in range(32)])  10.5 us
    ppermute x3, starting transfers between devices, over_tall(): return lax.ppermute(x, 'cel', [(i, i ^ WIDE * k) for i in range(32)])  8.69 us
    ppermute x11, waiting for transfers between devices, over_sta(): return lax.ppermute(x, 'sta', [(i, i ^ k) for i in range(8)])  5.44 us
    pallas_call x1, Pallas kernels, body(): pl.pallas_call(near_first_kernel, in_specs=[SMEM] * 2 + [HBM] * 2, out_sp...  3.25 us
    pallas_call x1, Pallas kernels, body(): pl.pallas_call(adjoint_kernel, in_specs=[SMEM] * 3 + [VMEM] * 5, out_spec...  2.54 us
    pallas_call x1, Pallas kernels, body(): pl.pallas_call(forward_kernel, in_specs=[SMEM] * 3 + [VMEM] * 12, out_spe...  2.54 us
  transfers between devices with their start and end apart: 14, of which 8 were waited for; matrix products, arithmetic and copies ran while one was open for 0% of the time, Pallas kernels for 4%

profile of v5, /device:TPU:1, one launch (start us, length us, event | category | flops | bytes accessed | tf_op | source)
XLA Modules:
  0.0 93.0 jit_solution(5202102022777091577)
XLA Ops:
  0.6 0.0 copy-start.4
  0.6 0.0 copy-start.5
  0.7 2.1 %collective-permute-start.1 = (bf16[2,8192]{1,0:T(2,128)(2,1)}, bf16[2,8192]{1,0:T(2,128)(2,1)S(1)}, u32[]{:S(2)}, u32[]{:S(2)}) collective-permute-start(bf16[2,8192]{1,0:T(2,128)(2,1)} %refs_0_.1), channel_id=1, source_target_pairs={{0,64},{32,96},{64,0},{96,32},{128,192},{160,224},{192,128},{224,1... | collective-permute-start | bytes 98312 | tf_op jit(solution)/shard_map/ppermute | solution.py:288
  2.8 2.5 %collective-permute-start.2 = (bf16[2,8192]{1,0:T(2,128)(2,1)}, bf16[2,8192]{1,0:T(2,128)(2,1)S(1)}, u32[]{:S(2)}, u32[]{:S(2)}) collective-permute-start(bf16[2,8192]{1,0:T(2,128)(2,1)} %refs_0_.1), channel_id=1, source_target_pairs={{0,128},{32,160},{64,192},{96,224},{128,0},{160,32},{192,64},{224,... | collective-permute-start | bytes 98312 | tf_op jit(solution)/shard_map/ppermute | solution.py:288
  5.2 0.0 collective-permute-start.3
  5.3 3.4 %collective-permute-start = (bf16[2,8192]{1,0:T(2,128)(2,1)}, bf16[2,8192]{1,0:T(2,128)(2,1)S(1)}, u32[]{:S(2)}, u32[]{:S(2)}) collective-permute-start(bf16[2,8192]{1,0:T(2,128)(2,1)} %refs_0_.1), channel_id=1, source_target_pairs={{0,32},{32,0},{64,96},{96,64},{128,160},{160,128},{192,224},{224,1... | collective-permute-start | bytes 98312 | tf_op jit(solution)/shard_map/ppermute | solution.py:288
  8.7 3.3 %near_first.1 = (bf16[32,256,256]{2,1,0:T(8,128)(2,1)S(1)}, bf16[32,256,48]{2,1,0:T(8,128)(2,1)S(1)}, f32[3,32768]{1,0:T(4,128)S(1)}) custom-call(s32[1,32]{1,0:T(1,128)} %counts.7, s32[2,64]{1,0:T(2,128)} %bitcast.18, f32[3,32768]{1,0:T(4,128)} %station_hbm.1, f32[3,8192]{1,0:T(4,128)} %cell_hbm.1), custom_call_target="tpu_custom_call" | custom-call | flops 402653184 | bytes 6291456 | tf_op jit(solution)/shard_map/near_first/pallas_call | solution.py:302
  11.9 0.0 collective-permute-done.1.refs_2_
  11.9 0.0 collective-permute-done.2.refs_4_
  12.0 0.0 collective-permute-done.3.refs_6_
  12.0 0.1 collective-permute-start.4
  12.1 0.5 collective-permute-start.5
  12.6 0.1 collective-permute-start.6
  12.7 0.0 copy-done.4
  12.7 0.0 copy-start.3
  12.7 0.0 copy-start.6
  12.7 0.6 near_second.1.refs_11_.second_blocks
  13.3 0.0 collective-permute-done.refs_1_
  13.3 0.0 collective-permute-done.4.refs_3_
  13.3 0.1 collective-permute-done.5.refs_5_
  13.4 0.3 collective-permute-done.6.refs_7_
  13.8 0.5 copy-done
  14.3 0.6 copy-done.1
  14.9 0.0 copy-done.3
  14.9 2.5 %forward.1 = bf16[32,16,1024]{2,1,0:T(8,128)(2,1)S(1)} custom-call(s32[1,32]{1,0:T(1,128)S(1)} %copy-done.5, s32[2,64]{1,0:T(2,128)S(1)} %bitcast.20, s32[2,128]{1,0:T(2,128)S(1)} %bitcast.22, bf16[2,8192]{1,0:T(2,128)(2,1)S(1)} %copy-done.3, bf16[2,8192]{1,0:T(2,128)(2,1)S(1)} %collective-permute-done.refs_1_, ...), custom_call_target="tpu_custom_call" | custom-call | tf_op jit(solution)/shard_map/forward/pallas_call | solution.py:336
  17.4 0.0 copy-start.2
  17.5 21.8 %all_to_all.10.parts = bf16[8,4,16,1024]{3,2,1,0:T(8,128)(2,1)S(1)} all-to-all(bf16[8,4,16,1024]{3,2,1,0:T(8,128)(2,1)S(1)} %bitcast.15), channel_id=1, replica_groups={{0,1,2,3,4,5,6,7},{8,9,10,11,12,13,14,15},{16,17,18,19,20,21,22,23},{24..., dimensions={0} | all-to-all | bytes 2097152 | tf_op jit(solution)/shard_map/all_to_all | solution.py:296
  39.2 0.1 share_sum.1.own
  39.4 4.4 %collective-permute-start.7 = (bf16[4,16,1024]{2,1,0:T(8,128)(2,1)S(1)}, bf16[4,16,1024]{2,1,0:T(8,128)(2,1)S(1)}, u32[]{:S(2)}, u32[]{:S(2)}) collective-permute-start(bf16[4,16,1024]{2,1,0:T(8,128)(2,1)S(1)} %share_sum.1.own), channel_id=1, source_target_pairs={{0,8},{1,9},{2,10},{3,11},{4,12},{5,13},{6,14},{7,15},{8,0},{9,1},... | collective-permute-start | bytes 393224 | tf_op jit(solution)/shard_map/ppermute | solution.py:293
  43.7 4.1 %collective-permute-start.8 = (bf16[4,16,1024]{2,1,0:T(8,128)(2,1)S(1)}, bf16[4,16,1024]{2,1,0:T(8,128)(2,1)S(1)}, u32[]{:S(2)}, u32[]{:S(2)}) collective-permute-start(bf16[4,16,1024]{2,1,0:T(8,128)(2,1)S(1)} %share_sum.1.own), channel_id=1, source_target_pairs={{0,16},{1,17},{2,18},{3,19},{4,20},{5,21},{6,22},{7,23},{8,24},{9,... | collective-permute-start | bytes 393224 | tf_op jit(solution)/shard_map/ppermute | solution.py:293
  47.9 0.2 collective-permute-start.9
  48.1 1.9 %collective-permute-done.7.one = bf16[4,16,1024]{2,1,0:T(8,128)(2,1)S(1)} collective-permute-done((bf16[4,16,1024]{2,1,0:T(8,128)(2,1)S(1)}, bf16[4,16,1024]{2,1,0:T(8,128)(2,1)S(1)}, u32[]{:S(2)}, u32[]{:S(2)}) %collective-permute-start.7) | collective-permute-done | bytes 131104 | tf_op jit(solution)/shard_map/ppermute | solution.py:293
  50.0 2.0 %collective-permute-done.8.two = bf16[4,16,1024]{2,1,0:T(8,128)(2,1)S(1)} collective-permute-done((bf16[4,16,1024]{2,1,0:T(8,128)(2,1)S(1)}, bf16[4,16,1024]{2,1,0:T(8,128)(2,1)S(1)}, u32[]{:S(2)}, u32[]{:S(2)}) %collective-permute-start.8) | collective-permute-done | bytes 131104 | tf_op jit(solution)/shard_map/ppermute | solution.py:293
  52.0 6.5 %collective-permute-done.9.three = bf16[4,16,1024]{2,1,0:T(8,128)(2,1)S(1)} collective-permute-done((bf16[4,16,1024]{2,1,0:T(8,128)(2,1)S(1)}, bf16[4,16,1024]{2,1,0:T(8,128)(2,1)S(1)}, u32[]{:S(2)}, u32[]{:S(2)}) %collective-permute-start.9) | collective-permute-done | bytes 131104 | tf_op jit(solution)/shard_map/ppermute | solution.py:293
  58.5 0.0 copy-done.2
  58.5 0.9 weigh.1
  59.4 16.7 %all_to_all.11 = bf16[8,4,16,1024]{3,2,1,0:T(8,128)(2,1)S(1)} all-to-all(bf16[8,4,16,1024]{3,2,1,0:T(8,128)(2,1)S(1)} %get-tuple-element.25), channel_id=1, replica_groups={{0,1,2,3,4,5,6,7},{8,9,10,11,12,13,14,15},{16,17,18,19,20,21,22,23},{24..., dimensions={0} | all-to-all | bytes 2097152 | tf_op jit(solution)/shard_map/all_to_all | solution.py:296
  76.1 2.5 %adjoint.1 = (f32[8,8192]{1,0:T(8,128)S(1)}, bf16[8,8192]{1,0:T(8,128)(2,1)S(1)}) custom-call(s32[1,32]{1,0:T(1,128)S(1)} %copy-done.5, s32[2,64]{1,0:T(2,128)S(1)} %bitcast.21, s32[2,128]{1,0:T(2,128)S(1)} %bitcast.23, bf16[32,16,1024]{2,1,0:T(8,128)(2,1)S(1)} %bitcast.16, bf16[16,256,256]{2,1,0:T(8,128)(2,1)S(1)} %bitcast.12, ...), custom_call_target="tpu_custom_call" | custom-call | tf_op jit(solution)/shard_map/adjoint/pallas_call | solution.py:369
  78.6 3.7 %collective-permute-start.10 = (bf16[8,8192]{1,0:T(8,128)(2,1)S(1)}, bf16[8,8192]{1,0:T(8,128)(2,1)S(1)}, u32[]{:S(2)}, u32[]{:S(2)}) collective-permute-start(bf16[8,8192]{1,0:T(8,128)(2,1)S(1)} %get-tuple-element.27), channel_id=1, source_target_pairs={{0,32},{32,0},{64,96},{96,64},{128,160},{160,128},{192,224},{224,1... | collective-permute-start | bytes 393224 | tf_op jit(solution)/shard_map/ppermute | solution.py:288
  82.3 1.0 %collective-permute-done.10.swapped = bf16[8,8192]{1,0:T(8,128)(2,1)S(1)} collective-permute-done((bf16[8,8192]{1,0:T(8,128)(2,1)S(1)}, bf16[8,8192]{1,0:T(8,128)(2,1)S(1)}, u32[]{:S(2)}, u32[]{:S(2)}) %collective-permute-start.10) | collective-permute-done | bytes 131104 | tf_op jit(solution)/shard_map/ppermute | solution.py:288
  83.3 0.1 chip_sum.1
  83.4 0.1 collective-permute-start.11
  83.5 4.9 %collective-permute-start.12 = (bf16[2,8192]{1,0:T(2,128)(2,1)S(1)}, bf16[2,8192]{1,0:T(2,128)(2,1)S(1)}, u32[]{:S(2)}, u32[]{:S(2)}) collective-permute-start(bf16[2,8192]{1,0:T(2,128)(2,1)S(1)} %get-tuple-element.30), channel_id=1, source_target_pairs={{0,128},{32,160},{64,192},{96,224},{128,0},{160,32},{192,64},{224,... | collective-permute-start | bytes 98312 | tf_op jit(solution)/shard_map/ppermute | solution.py:288
  88.3 0.0 collective-permute-start.13
  88.3 0.0 collective-permute-done.11
  88.4 1.6 %collective-permute-done.12 = bf16[2,8192]{1,0:T(2,128)(2,1)S(1)} collective-permute-done((bf16[2,8192]{1,0:T(2,128)(2,1)S(1)}, bf16[2,8192]{1,0:T(2,128)(2,1)S(1)}, u32[]{:S(2)}, u32[]{:S(2)}) %collective-permute-start.12) | collective-permute-done | bytes 32800 | tf_op jit(solution)/shard_map/ppermute | solution.py:288
  90.0 2.3 %collective-permute-done.13 = bf16[2,8192]{1,0:T(2,128)(2,1)S(1)} collective-permute-done((bf16[2,8192]{1,0:T(2,128)(2,1)S(1)}, bf16[2,8192]{1,0:T(2,128)(2,1)S(1)}, u32[]{:S(2)}, u32[]{:S(2)}) %collective-permute-start.13) | collective-permute-done | bytes 32800 | tf_op jit(solution)/shard_map/ppermute | solution.py:288
  92.3 0.7 convert_add_fusion
  (4 shorter events, 0.0 us)
Async XLA Ops:
  0.6 12.0 %copy-start.4 = (s32[1,1,64,2]{2,3,1,0:T(2,128)S(1)}, s32[1,1,64,2]{2,3,1,0:T(2,128)}, u32[]{:S(2)}) copy-start(s32[1,1,64,2]{2,3,1,0:T(2,128)} %param.13) | copy-start | bytes 1540
  0.6 12.0 %copy-start.5 = (s32[1,32]{1,0:T(1,128)S(1)}, s32[1,32]{1,0:T(1,128)}, u32[]{:S(2)}) copy-start(s32[1,32]{1,0:T(1,128)} %counts.7) | copy-start | bytes 388
  0.7 11.3 %collective-permute-start.1 = (bf16[2,8192]{1,0:T(2,128)(2,1)}, bf16[2,8192]{1,0:T(2,128)(2,1)S(1)}, u32[]{:S(2)}, u32[]{:S(2)}) collective-permute-start(bf16[2,8192]{1,0:T(2,128)(2,1)} %refs_0_.1), channel_id=1, source_target_pairs={{0,64},{32,96},{64,0},{96,32},{128,192},{160,224},{192,128},{224,1... | collective-permute-start | bytes 98312 | tf_op jit(solution)/shard_map/ppermute | solution.py:288
  2.8 9.2 %collective-permute-start.2 = (bf16[2,8192]{1,0:T(2,128)(2,1)}, bf16[2,8192]{1,0:T(2,128)(2,1)S(1)}, u32[]{:S(2)}, u32[]{:S(2)}) collective-permute-start(bf16[2,8192]{1,0:T(2,128)(2,1)} %refs_0_.1), channel_id=1, source_target_pairs={{0,128},{32,160},{64,192},{96,224},{128,0},{160,32},{192,64},{224,... | collective-permute-start | bytes 98312 | tf_op jit(solution)/shard_map/ppermute | solution.py:288
  5.2 6.7 %collective-permute-start.3 = (bf16[2,8192]{1,0:T(2,128)(2,1)}, bf16[2,8192]{1,0:T(2,128)(2,1)S(1)}, u32[]{:S(2)}, u32[]{:S(2)}) collective-permute-start(bf16[2,8192]{1,0:T(2,128)(2,1)} %refs_0_.1), channel_id=1, source_target_pairs={{0,192},{32,224},{64,128},{96,160},{128,64},{160,96},{192,0},{224,... | collective-permute-start | bytes 98312 | tf_op jit(solution)/shard_map/ppermute | solution.py:288
  5.3 8.0 %collective-permute-start = (bf16[2,8192]{1,0:T(2,128)(2,1)}, bf16[2,8192]{1,0:T(2,128)(2,1)S(1)}, u32[]{:S(2)}, u32[]{:S(2)}) collective-permute-start(bf16[2,8192]{1,0:T(2,128)(2,1)} %refs_0_.1), channel_id=1, source_target_pairs={{0,32},{32,0},{64,96},{96,64},{128,160},{160,128},{192,224},{224,1... | collective-permute-start | bytes 98312 | tf_op jit(solution)/shard_map/ppermute | solution.py:288
  12.0 1.3 %collective-permute-start.4 = (bf16[2,8192]{1,0:T(2,128)(2,1)S(1)}, bf16[2,8192]{1,0:T(2,128)(2,1)S(1)}, u32[]{:S(2)}, u32[]{:S(2)}) collective-permute-start(bf16[2,8192]{1,0:T(2,128)(2,1)S(1)} %collective-permute-done.1.refs_2_), channel_id=1, source_target_pairs={{0,32},{32,0},{64,96},{96,64},{128,160},{160,128},{192,224},{224,1... | collective-permute-start | bytes 98312 | tf_op jit(solution)/shard_map/ppermute | solution.py:288
  12.1 1.4 %collective-permute-start.5 = (bf16[2,8192]{1,0:T(2,128)(2,1)S(1)}, bf16[2,8192]{1,0:T(2,128)(2,1)S(1)}, u32[]{:S(2)}, u32[]{:S(2)}) collective-permute-start(bf16[2,8192]{1,0:T(2,128)(2,1)S(1)} %collective-permute-done.2.refs_4_), channel_id=1, source_target_pairs={{0,32},{32,0},{64,96},{96,64},{128,160},{160,128},{192,224},{224,1... | collective-permute-start | bytes 98312 | tf_op jit(solution)/shard_map/ppermute | solution.py:288
  12.6 1.2 %collective-permute-start.6 = (bf16[2,8192]{1,0:T(2,128)(2,1)S(1)}, bf16[2,8192]{1,0:T(2,128)(2,1)S(1)}, u32[]{:S(2)}, u32[]{:S(2)}) collective-permute-start(bf16[2,8192]{1,0:T(2,128)(2,1)S(1)} %collective-permute-done.3.refs_6_), channel_id=1, source_target_pairs={{0,32},{32,0},{64,96},{96,64},{128,160},{160,128},{192,224},{224,1... | collective-permute-start | bytes 98312 | tf_op jit(solution)/shard_map/ppermute | solution.py:288
  12.7 1.6 %copy-start = (bf16[1,1,128,32,256]{4,3,2,1,0:T(8,128)(2,1)S(1)}, bf16[1,1,128,32,256]{4,3,2,1,0:T(8,128)(2,1)}, u32[]{:S(2)}) copy-start(bf16[1,1,128,32,256]{4,3,2,1,0:T(8,128)(2,1)} %param.16) | copy-start | bytes 6291460
  12.7 2.2 %copy-start.1 = (bf16[1,1,128,32,256]{4,3,2,1,0:T(8,128)(2,1)S(1)}, bf16[1,1,128,32,256]{4,3,2,1,0:T(8,128)(2,1)}, u32[]{:S(2)}) copy-start(bf16[1,1,128,32,256]{4,3,2,1,0:T(8,128)(2,1)} %param.17) | copy-start | bytes 6291460
  12.7 2.2 %copy-start.3 = (bf16[2,8192]{1,0:T(2,128)(2,1)S(1)}, bf16[2,8192]{1,0:T(2,128)(2,1)}, u32[]{:S(2)}) copy-start(bf16[2,8192]{1,0:T(2,128)(2,1)} %refs_0_.1) | copy-start | bytes 98308
  12.7 2.2 %copy-start.6 = (s32[1,1,128,2]{2,3,1,0:T(2,128)S(1)}, s32[1,1,128,2]{2,3,1,0:T(2,128)}, u32[]{:S(2)}) copy-start(s32[1,1,128,2]{2,3,1,0:T(2,128)} %param.15) | copy-start | bytes 3076
  17.4 41.1 %copy-start.2 = (f32[32768]{0:T(1024)S(1)}, f32[32768]{0:T(1024)}, u32[]{:S(2)}) copy-start(f32[32768]{0:T(1024)} %param.12) | copy-start | bytes 393220
  39.4 10.6 %collective-permute-start.7 = (bf16[4,16,1024]{2,1,0:T(8,128)(2,1)S(1)}, bf16[4,16,1024]{2,1,0:T(8,128)(2,1)S(1)}, u32[]{:S(2)}, u32[]{:S(2)}) collective-permute-start(bf16[4,16,1024]{2,1,0:T(8,128)(2,1)S(1)} %share_sum.1.own), channel_id=1, source_target_pairs={{0,8},{1,9},{2,10},{3,11},{4,12},{5,13},{6,14},{7,15},{8,0},{9,1},... | collective-permute-start | bytes 393224 | tf_op jit(solution)/shard_map/ppermute | solution.py:293
  43.7 8.2 %collective-permute-start.8 = (bf16[4,16,1024]{2,1,0:T(8,128)(2,1)S(1)}, bf16[4,16,1024]{2,1,0:T(8,128)(2,1)S(1)}, u32[]{:S(2)}, u32[]{:S(2)}) collective-permute-start(bf16[4,16,1024]{2,1,0:T(8,128)(2,1)S(1)} %share_sum.1.own), channel_id=1, source_target_pairs={{0,16},{1,17},{2,18},{3,19},{4,20},{5,21},{6,22},{7,23},{8,24},{9,... | collective-permute-start | bytes 393224 | tf_op jit(solution)/shard_map/ppermute | solution.py:293
  47.9 10.6 %collective-permute-start.9 = (bf16[4,16,1024]{2,1,0:T(8,128)(2,1)S(1)}, bf16[4,16,1024]{2,1,0:T(8,128)(2,1)S(1)}, u32[]{:S(2)}, u32[]{:S(2)}) collective-permute-start(bf16[4,16,1024]{2,1,0:T(8,128)(2,1)S(1)} %share_sum.1.own), channel_id=1, source_target_pairs={{0,24},{1,25},{2,26},{3,27},{4,28},{5,29},{6,30},{7,31},{8,16},{9,... | collective-permute-start | bytes 393224 | tf_op jit(solution)/shard_map/ppermute | solution.py:293
  78.6 4.7 %collective-permute-start.10 = (bf16[8,8192]{1,0:T(8,128)(2,1)S(1)}, bf16[8,8192]{1,0:T(8,128)(2,1)S(1)}, u32[]{:S(2)}, u32[]{:S(2)}) collective-permute-start(bf16[8,8192]{1,0:T(8,128)(2,1)S(1)} %get-tuple-element.27), channel_id=1, source_target_pairs={{0,32},{32,0},{64,96},{96,64},{128,160},{160,128},{192,224},{224,1... | collective-permute-start | bytes 393224 | tf_op jit(solution)/shard_map/ppermute | solution.py:288
  83.4 5.0 %collective-permute-start.11 = (bf16[2,8192]{1,0:T(2,128)(2,1)S(1)}, bf16[2,8192]{1,0:T(2,128)(2,1)S(1)}, u32[]{:S(2)}, u32[]{:S(2)}) collective-permute-start(bf16[2,8192]{1,0:T(2,128)(2,1)S(1)} %get-tuple-element.29), channel_id=1, source_target_pairs={{0,64},{32,96},{64,0},{96,32},{128,192},{160,224},{192,128},{224,1... | collective-permute-start | bytes 98312 | tf_op jit(solution)/shard_map/ppermute | solution.py:288
  83.5 6.5 %collective-permute-start.12 = (bf16[2,8192]{1,0:T(2,128)(2,1)S(1)}, bf16[2,8192]{1,0:T(2,128)(2,1)S(1)}, u32[]{:S(2)}, u32[]{:S(2)}) collective-permute-start(bf16[2,8192]{1,0:T(2,128)(2,1)S(1)} %get-tuple-element.30), channel_id=1, source_target_pairs={{0,128},{32,160},{64,192},{96,224},{128,0},{160,32},{192,64},{224,... | collective-permute-start | bytes 98312 | tf_op jit(solution)/shard_map/ppermute | solution.py:288
  88.3 4.0 %collective-permute-start.13 = (bf16[2,8192]{1,0:T(2,128)(2,1)S(1)}, bf16[2,8192]{1,0:T(2,128)(2,1)S(1)}, u32[]{:S(2)}, u32[]{:S(2)}) collective-permute-start(bf16[2,8192]{1,0:T(2,128)(2,1)S(1)} %get-tuple-element.31), channel_id=1, source_target_pairs={{0,192},{32,224},{64,128},{96,160},{128,64},{160,96},{192,0},{224,... | collective-permute-start | bytes 98312 | tf_op jit(solution)/shard_map/ppermute | solution.py:288
